TPU v7x, 32 devices: a whole 2x2x4 slice. The times are simulated.
32 devices in a mesh: fsdp: 8 (over z, y), tp: 4 (over x, core).
Axes of the slice: x: 2, y: 2, z: 4, core: 2. Of those that a mesh axis runs over, the one named last changes fastest.
Arguments:
- base_weight: bfloat16 [16384, 26624], P(('fsdp', 'tp')), may hold values from -0.09375 to 0.09375
- left_factor: bfloat16 [16384, 64], P(('fsdp', 'tp')), may hold values from -0.75 to 0.75
- right_factor: bfloat16 [64, 26624], P(None, 'tp'), may hold values from -0.029907227 to 0.029907227
- magnitude: float32 [26624], replicated, may hold values from 6 to 96
Outputs:
- quantized: bfloat16 [16384, 26624], P('fsdp', 'tp')
- block_scales: float32 [128, 208], P('fsdp', 'tp')
All inputs are finite; a program needn't handle non-finite values. Where the computation divides by a largest or mean magnitude, that divisor is 1e-20 or more.
Results may differ from a plain program's by a relative error of at most 0.01.
Values may be sent and summed in bfloat16 or wider, within the bound.
No kernel may reach another device: no remote copies, remote signals or barrier semaphores. Data moves between devices by JAX's collectives and lax.ppermute only.
A program may use at most 320 MiB of HBM per device.

v0:
```python
import jax
import jax.numpy as jnp
from jax import lax
from jax.sharding import PartitionSpec as P

BLOCK = 128


epsilon = 1e-06


def to_blocks(merged):
    row_count, col_count = merged.shape
    tile_view = merged.astype(jnp.float32).reshape(
        row_count // BLOCK, BLOCK, col_count // BLOCK, BLOCK
    )
    block_max = jnp.max(jnp.abs(tile_view), axis=(1, 3))
    scaled = tile_view / (block_max[:, None, :, None] + epsilon)
    return (scaled.astype(jnp.bfloat16).reshape(row_count, col_count), block_max)


def body(base_weight, left_factor, right_factor, magnitude):
    frozen = lax.all_to_all(base_weight, "tp", split_axis=1, concat_axis=0, tiled=True)
    low_rank = jnp.dot(
        lax.all_gather(left_factor, "tp", axis=0, tiled=True),
        right_factor,
        preferred_element_type=jnp.float32,
    )
    combined = frozen.astype(jnp.float32) + low_rank
    col_squares = lax.psum(jnp.sum(combined * combined, axis=0), "fsdp")
    col_count = combined.shape[1]
    mag_cols = lax.dynamic_slice_in_dim(magnitude, lax.axis_index("tp") * col_count, col_count, 0)
    served = (mag_cols * combined / jnp.sqrt(col_squares + epsilon)).astype(jnp.bfloat16)
    quantized, block_scales = to_blocks(served)
    return (quantized, block_scales)


def solution(mesh):
    in_specs = (P(("fsdp", "tp"), None), P(("fsdp", "tp"), None), P(None, "tp"), P())
    out_specs = (P("fsdp", "tp"), P("fsdp", "tp"))
    return jax.shard_map(body, mesh=mesh, in_specs=in_specs, out_specs=out_specs, check_vma=False)
```

profile of v0, /device:TPU:0, one launch (start us, length us, event | category | flops | bytes accessed | tf_op | source)
XLA Modules:
  0.0 655.2 jit_solution(524163815536215362)
XLA Ops:
  0.6 0.0 copy-start
  0.6 0.0 copy-start.2
  0.7 19.5 %copy.22 = bf16[64,4,8,6656]{3,2,0,1:T(8,128)(2,1)} copy(bf16[64,4,8,6656]{3,2,1,0:T(8,128)(2,1)} %bitcast.20) | data formatting | bytes 54525952 | tf_op jit(solution)/shard_map/all_to_all | solution.py:23
  20.1 8.7 %all-to-all-start = ((bf16[512,4,6656]{2,0,1:T(8,128)(2,1)}), bf16[512,4,6656]{2,0,1:T(8,128)(2,1)}, u32[]{:S(2)}, u32[]{:S(2)}) async-start(bf16[512,4,6656]{2,0,1:T(8,128)(2,1)} %bitcast.19), calls=%async_computation | async-start | bytes 54525952 | tf_op jit(solution)/shard_map/all_to_all | solution.py:23
  28.9 0.8 dynamic_slice.3
  29.7 0.0 copy-done.2
  29.7 297.3 %all_gather.3 = bf16[2048,64]{0,1:T(8,128)(2,1)S(1)} all-gather(bf16[512,64]{0,1:T(8,128)(2,1)S(1)} %copy-done.2), channel_id=1, replica_groups=mesh['fsdp'=8,'tp'=4] {'tp'}, dimensions={0}, use_global_device_ids=true | all-gather | bytes 327680 | tf_op jit(solution)/shard_map/all_gather | solution.py:25
  327.1 0.0 all-to-all-done
  327.1 0.0 copy-done
  327.1 27.3 %multiply_reduce_fusion = (f32[6656]{0:T(1024)S(1)}, f32[2048,6656]{1,0:T(8,128)}) fusion(bf16[2048,64]{0,1:T(8,128)(2,1)S(1)} %all_gather.3, bf16[64,6656]{1,0:T(8,128)(2,1)S(1)} %copy-done, bf16[512,4,6656]{2,0,1:T(8,128)(2,1)} %all-to-all-done), kind=kOutput, calls=%fused_computation.6 | convolution fusion | flops 1799349760 | bytes 82929664 | tf_op jit(solution)/shard_map/dot_general | solution.py:24
  354.4 38.2 %psum.7 = f32[6656]{0:T(1024)S(1)} all-reduce(f32[6656]{0:T(1024)S(1)} %get-tuple-element.4), channel_id=1, replica_groups=mesh['fsdp'=8,'tp'=4] {'fsdp'}, use_global_device_ids=true, to_apply=%region_1.0 | all-reduce | flops 6656 | bytes 53248 | tf_op jit(solution)/shard_map/psum | solution.py:30
  392.6 35.9 %convert_abs_fusion = f32[2048,6656]{1,0:T(8,128)} fusion(f32[6656]{0:T(1024)S(1)} %add_sqrt_fusion, f32[2048,6656]{1,0:T(8,128)} %get-tuple-element.5, f32[6656]{0:T(1024)S(1)} %dynamic_slice.3), kind=kLoop, calls=%fused_computation.1 | loop fusion | flops 68157440 | bytes 109105152 | tf_op jit(solution)/shard_map/abs | solution.py:17
  428.5 58.7 %reshape.20 = f32[16,128,52,128]{3,2,1,0:T(8,128)} reshape(f32[2048,6656]{1,0:T(8,128)} %convert_abs_fusion) | data formatting | bytes 109051904 | tf_op jit(solution)/shard_map/abs | solution.py:17
  487.2 18.3 %reduce_max.9 = f32[16,52]{1,0:T(8,128)S(1)} reduce(f32[16,128,52,128]{3,2,1,0:T(8,128)} %reshape.20, f32[]{:T(128)} %constant.5.clone.1), dimensions={1,3}, to_apply=%region_2.0 | reduce | flops 13630656 | bytes 54529284 | tf_op jit(solution)/shard_map/reduce_max | solution.py:17
  505.5 0.0 copy-start.3
  505.5 0.1 copy.16
  505.6 17.6 %div.21 = f32[16,128,52,128]{1,0,3,2:T(8,128)} broadcast(f32[16,52]{0,1:T(8,128)S(1)} %broadcast_add_fusion), dimensions={0,2} | broadcast | bytes 54529280 | tf_op jit(solution)/shard_map/div | solution.py:18
  523.3 37.6 %copy.21 = f32[832,8,16,128]{3,1,2,0:T(8,128)} copy(f32[832,8,16,128]{3,2,1,0:T(8,128)} %bitcast.17) | data formatting | bytes 109051904
  560.9 0.0 copy-done.3
  560.9 0.0 copy-start.1
  560.9 50.1 %copy.13 = f32[2048,6656]{1,0:T(8,128)} copy(f32[2048,6656]{0,1:T(8,128)} %bitcast.18) | data formatting | bytes 109051904 | tf_op jit(solution)/shard_map/div | solution.py:18
  611.0 44.2 %fusion = bf16[2048,6656]{1,0:T(8,128)(2,1)} fusion(f32[2048,6656]{1,0:T(8,128)} %copy.13, f32[6656]{0:T(1024)S(1)} %add_sqrt_fusion, f32[2048,6656]{1,0:T(8,128)} %get-tuple-element.5, f32[6656]{0:T(1024)S(1)} %dynamic_slice.3), kind=kLoop, calls=%fused_computation.2 | loop fusion | flops 81788928 | bytes 136368128 | tf_op jit(solution)/shard_map/convert_element_type | solution.py:19
  655.2 0.0 copy-done.1
  (2 shorter events, 0.0 us)
Async XLA Ops:
  0.6 326.4 %copy-start = (bf16[64,6656]{1,0:T(8,128)(2,1)S(1)}, bf16[64,6656]{1,0:T(8,128)(2,1)}, u32[]{:S(2)}) copy-start(bf16[64,6656]{1,0:T(8,128)(2,1)} %param.6) | copy-start | bytes 2555908
  0.6 29.1 %copy-start.2 = (bf16[512,64]{0,1:T(8,128)(2,1)S(1)}, bf16[512,64]{0,1:T(8,128)(2,1)}, u32[]{:S(2)}) copy-start(bf16[512,64]{0,1:T(8,128)(2,1)} %param.5) | copy-start | bytes 196612
  20.1 306.9 %all-to-all-start = ((bf16[512,4,6656]{2,0,1:T(8,128)(2,1)}), bf16[512,4,6656]{2,0,1:T(8,128)(2,1)}, u32[]{:S(2)}, u32[]{:S(2)}) async-start(bf16[512,4,6656]{2,0,1:T(8,128)(2,1)} %bitcast.19), calls=%async_computation | async-start | bytes 54525952 | tf_op jit(solution)/shard_map/all_to_all | solution.py:23
  505.5 55.4 %copy-start.3 = (f32[16,52]{1,0:T(8,128)}, f32[16,52]{1,0:T(8,128)S(1)}, u32[]{:S(2)}) copy-start(f32[16,52]{1,0:T(8,128)S(1)} %reduce_max.9) | copy-start | bytes 9988
  560.9 94.3 %copy-start.1 = (bf16[64,6656]{1,0:T(8,128)(2,1)S(1)}, bf16[64,6656]{1,0:T(8,128)(2,1)}, u32[]{:S(2)}) copy-start(bf16[64,6656]{1,0:T(8,128)(2,1)} %param.6) | copy-start | bytes 2555908
where the time goes:
time: 658 us; the launch traced here: 655 us
  blocking collectives  336 us (51%)
  local copies, waits for them, and re-layouts  184 us (28%)
  other arithmetic  98.5 us (15%)
  matrix products  27.3 us (4%)
  starting transfers between devices  8.74 us (1%)
    all_gather x1, blocking collectives, body(): lax.all_gather(left_factor, 'tp', axis=0, tiled=True)  297 us
    div x2, local copies, waits for them, and re-layouts, to_blocks(): scaled = tile_view / (block_max[:, None, :, None] + epsilon)  67.7 us
    abs x1, local copies, waits for them, and re-layouts, to_blocks(): block_max = jnp.max(jnp.abs(tile_view), axis=(1, 3))  58.7 us
    convert_element_type x1, other arithmetic, to_blocks(): scaled.astype(jnp.bfloat16).reshape(row_count, col_count)  44.2 us
    psum x1, blocking collectives, body(): col_squares = lax.psum(jnp.sum(combined * combined, axis=0), 'fsdp')  38.2 us
    unnamed x10, local copies, waits for them, and re-layouts  37.7 us
    abs x1, other arithmetic, to_blocks(): block_max = jnp.max(jnp.abs(tile_view), axis=(1, 3))  35.9 us
    dot_general x1, matrix products, body(): jnp.dot(lax.all_gather(left_factor, 'tp', axis=0, tiled=True), right_fact...  27.3 us
  transfers between devices with their start and end apart: 1, of which 0 were waited for; matrix products, arithmetic and copies ran while one was open for 0% of the time, Pallas kernels for 0%

commit v1 on v0

v1 whole, which is shorter than its diff:
```python
import functools

import jax
import jax.numpy as jnp
from jax import lax
from jax.experimental import pallas as pl
from jax.experimental.pallas import tpu as pltpu
from jax.sharding import PartitionSpec as P

BLOCK = 128
EPSILON = 1e-06
PARTS = (2, 3, 3, 3, 2)


def chunk_units(total, parts):
    bounds = [0]
    whole = sum(parts)
    for i in range(len(parts)):
        bounds.append(round(total * sum(parts[: i + 1]) / whole))
    return [(a, b) for a, b in zip(bounds, bounds[1:]) if b > a]


def pack_kernel(base_ref, out_ref):
    out_ref[...] = base_ref[...]


def pack(base, tp, unit, first, count):
    rows = base.shape[0]
    group_units = base.shape[1] // (tp * unit)
    return pl.pallas_call(
        pack_kernel,
        out_shape=jax.ShapeDtypeStruct((tp * rows, count * unit), base.dtype),
        grid=(tp, count),
        in_specs=[pl.BlockSpec((rows, unit), lambda g, j: (0, g * group_units + first + j))],
        out_specs=pl.BlockSpec((rows, unit), lambda g, j: (g, j)),
        compiler_params=pltpu.CompilerParams(vmem_limit_bytes=40 * 2**20),
        cost_estimate=pl.CostEstimate(
            flops=0, bytes_accessed=4 * tp * rows * count * unit, transcendentals=0
        ),
    )(base)


def squares_kernel(piece_ref, left_ref, right_ref, out_ref):
    rows, cols = piece_ref.shape
    total = jnp.zeros((8, cols), jnp.float32)
    for r in range(0, rows, BLOCK):
        span = pl.ds(r, BLOCK)
        low_rank = jnp.dot(left_ref[span, :], right_ref[...], preferred_element_type=jnp.float32)
        combined = piece_ref[span, :].astype(jnp.float32) + low_rank
        squares = combined * combined
        total = total + jnp.sum(squares.reshape(BLOCK // 8, 8, cols), axis=0)
    out_ref[...] = jnp.sum(total, axis=0, keepdims=True)


def column_squares(piece, left, right, unit, first):
    rows, cols = piece.shape
    rank = left.shape[1]
    return pl.pallas_call(
        squares_kernel,
        out_shape=jax.ShapeDtypeStruct((1, cols), jnp.float32),
        grid=(cols // unit,),
        in_specs=[
            pl.BlockSpec((rows, unit), lambda j: (0, j)),
            pl.BlockSpec((rows, rank), lambda j: (0, 0)),
            pl.BlockSpec((rank, unit), lambda j: (0, first + j)),
        ],
        out_specs=pl.BlockSpec((1, unit), lambda j: (0, j)),
        compiler_params=pltpu.CompilerParams(vmem_limit_bytes=40 * 2**20),
        cost_estimate=pl.CostEstimate(
            flops=2 * rows * cols * rank, bytes_accessed=2 * rows * cols, transcendentals=0
        ),
    )(piece, left, right)


def export_kernel(first, piece_ref, left_ref, right_ref, squares_ref, mag_ref, *rest):
    out_ref, scales_ref = rest[-2:]
    rows, cols = piece_ref.shape
    step = pl.program_id(0)
    if len(rest) > 2:
        @pl.when(step == 0)
        def _():
            scales_ref[...] = rest[1][...]

    factor = mag_ref[...] / jnp.sqrt(squares_ref[...] + EPSILON)
    lane = lax.broadcasted_iota(jnp.int32, (1, scales_ref.shape[1]), 1)
    per_step = cols // BLOCK
    for i in range(rows // BLOCK):
        span = pl.ds(i * BLOCK, BLOCK)
        low_rank = jnp.dot(left_ref[span, :], right_ref[...], preferred_element_type=jnp.float32)
        combined = piece_ref[span, :].astype(jnp.float32) + low_rank
        merged = (combined * factor).astype(jnp.bfloat16).astype(jnp.float32)
        line = scales_ref[pl.ds(i, 1), :]
        for j in range(per_step):
            tile = merged[:, j * BLOCK : (j + 1) * BLOCK]
            largest = jnp.max(jnp.max(jnp.abs(tile), axis=0, keepdims=True), axis=1, keepdims=True)
            out_ref[span, pl.ds(j * BLOCK, BLOCK)] = (tile * (1.0 / (largest + EPSILON))).astype(jnp.bfloat16)
            line = jnp.where(lane == (first + step) * per_step + j, largest, line)
        scales_ref[pl.ds(i, 1), :] = line


def export_chunk(piece, left, right, squares, mag, unit, first, previous):
    rows, cols = piece.shape
    rank, all_cols = right.shape
    scale_shape = (rows // BLOCK, all_cols // BLOCK)
    in_specs = [
        pl.BlockSpec((rows, unit), lambda j: (0, j)),
        pl.BlockSpec((rows, rank), lambda j: (0, 0)),
        pl.BlockSpec((rank, unit), lambda j: (0, first + j)),
        pl.BlockSpec((1, unit), lambda j: (0, j)),
        pl.BlockSpec((1, unit), lambda j: (0, first + j)),
    ]
    args = [piece, left, right, squares, mag]
    aliases = {}
    if previous is not None:
        in_specs += [pl.BlockSpec(memory_space=pl.ANY), pl.BlockSpec(scale_shape, lambda j: (0, 0))]
        args += list(previous)
        aliases = {5: 0, 6: 1}
    return pl.pallas_call(
        functools.partial(export_kernel, first),
        out_shape=(
            jax.ShapeDtypeStruct((rows, all_cols), jnp.bfloat16),
            jax.ShapeDtypeStruct(scale_shape, jnp.float32),
        ),
        grid=(cols // unit,),
        in_specs=in_specs,
        out_specs=(
            pl.BlockSpec((rows, unit), lambda j: (0, first + j)),
            pl.BlockSpec(scale_shape, lambda j: (0, 0)),
        ),
        input_output_aliases=aliases,
        compiler_params=pltpu.CompilerParams(vmem_limit_bytes=40 * 2**20),
        cost_estimate=pl.CostEstimate(
            flops=2 * rows * cols * rank, bytes_accessed=4 * rows * cols, transcendentals=0
        ),
    )(*args)


def body(tp, base_weight, left_factor, right_factor, magnitude):
    rows, rank = left_factor.shape
    cols = right_factor.shape[1]
    blocks = cols // BLOCK
    unit = max(d for d in (4, 2, 1) if blocks % d == 0) * BLOCK
    left = lax.all_gather(left_factor, "tp", axis=0, tiled=True)
    left, base_weight = lax.optimization_barrier((left, base_weight))
    mag = lax.dynamic_slice_in_dim(magnitude, lax.axis_index("tp") * cols, cols, 0).reshape(1, cols)
    result = squares = None
    for a, b in chunk_units(cols // unit, PARTS):
        packed = pack(base_weight, tp, unit, a, b - a)
        piece = lax.all_to_all(packed, "tp", split_axis=0, concat_axis=0, tiled=True)
        local = column_squares(piece, left, right_factor, unit, a)
        if squares is not None:
            local, _ = lax.optimization_barrier((local, squares))
        squares = lax.psum(local, "fsdp")
        result = export_chunk(piece, left, right_factor, squares, mag, unit, a, result)
    return result


def solution(mesh):
    in_specs = (P(("fsdp", "tp"), None), P(("fsdp", "tp"), None), P(None, "tp"), P())
    out_specs = (P("fsdp", "tp"), P("fsdp", "tp"))
    return jax.shard_map(
        functools.partial(body, mesh.shape["tp"]), mesh=mesh, in_specs=in_specs, out_specs=out_specs, check_vma=False
    )
```

time: 658 us -> 435 us (0.66)
  blocking collectives: 336 us -> 104 us
  waiting for transfers between devices: 0.01 us -> 202 us
  local copies, waits for them, and re-layouts: 184 us -> 13.7 us
  other arithmetic: 98.5 us -> 0 us
  Pallas kernels: 0 us -> 87.4 us
  matrix products: 27.3 us -> 0 us
  starting transfers between devices: 8.74 us -> 25.7 us
    all_gather x1, blocking collectives: 297 us -> 8.62 us  [body(): left = lax.all_gather(left_factor, 'tp', axis=0, tiled=True)]
    all_to_all x1 -> x5, waiting for transfers between devices: 0.01 us -> 202 us  [body(): lax.all_to_all(packed, 'tp', split_axis=0, concat_axis=0, tiled=True)]
    pallas_call x0 -> x15, Pallas kernels: none -> 87.4 us  [the longest x5 36.5 us: export_chunk(): pl.pallas_call(functools.partial(export_kernel, first), out_shape=(jax.Sh...]
    div x2 -> x0, local copies, waits for them, and re-layouts: 67.7 us -> none  [to_blocks(): scaled = tile_view / (block_max[:, None, :, None] + epsilon)]
    abs x1 -> x0, local copies, waits for them, and re-layouts: 58.7 us -> none  [to_blocks(): block_max = jnp.max(jnp.abs(tile_view), axis=(1, 3))]
    psum x1 -> x5, blocking collectives: 38.2 us -> 95.2 us  [body(): squares = lax.psum(local, 'fsdp')]
    convert_element_type x1 -> x0, other arithmetic: 44.2 us -> none  [to_blocks(): scaled.astype(jnp.bfloat16).reshape(row_count, col_count)]
    abs x1 -> x0, other arithmetic: 35.9 us -> none  [to_blocks(): block_max = jnp.max(jnp.abs(tile_view), axis=(1, 3))]
  transfers between devices with their start and end apart: 1 -> 5, of which waited for: 0 -> 4; matrix products, arithmetic and copies ran while one was open for 0% -> 0% of each run, Pallas kernels for 0% -> 11%
where the time goes in v1:
time: 435 us; the launch traced here: 433 us
  waiting for transfers between devices  202 us (46%)
  blocking collectives  104 us (24%)
  Pallas kernels  87.4 us (20%)
  starting transfers between devices  25.7 us (6%)
  local copies, waits for them, and re-layouts  13.7 us (3%)
    all_to_all x5, waiting for transfers between devices, body(): lax.all_to_all(packed, 'tp', split_axis=0, concat_axis=0, tiled=True)  202 us
    psum x5, blocking collectives, body(): squares = lax.psum(local, 'fsdp')  95.2 us
    pallas_call x5, Pallas kernels, export_chunk(): pl.pallas_call(functools.partial(export_kernel, first), out_shape=(jax.Sh...  36.5 us
    pallas_call x5, Pallas kernels, pack(): pl.pallas_call(pack_kernel, out_shape=jax.ShapeDtypeStruct((tp * rows, co...  31.1 us
    all_to_all x5, starting transfers between devices, body(): lax.all_to_all(packed, 'tp', split_axis=0, concat_axis=0, tiled=True)  25.7 us
    pallas_call x5, Pallas kernels, column_squares(): pl.pallas_call(squares_kernel, out_shape=jax.ShapeDtypeStruct((1, cols),...  19.9 us
    unnamed x13, local copies, waits for them, and re-layouts  12.8 us
  transfers between devices with their start and end apart: 5, of which 4 were waited for; matrix products, arithmetic and copies ran while one was open for 0% of the time, Pallas kernels for 11%

profile of v1, /device:TPU:0, one launch (start us, length us, event | category | flops | bytes accessed | tf_op | source)
XLA Modules:
  0.0 433.1 jit_solution(11094190647358841667)
XLA Ops:
  1.6 8.6 %all_gather.3.left_ref = bf16[2048,64]{1,0:T(8,128)(2,1)S(1)} all-gather(bf16[512,64]{1,0:T(8,128)(2,1)S(1)} %copy.14), channel_id=1, replica_groups=mesh['fsdp'=8,'tp'=4] {'tp'}, dimensions={0}, use_global_device_ids=true | all-gather | bytes 327680 | tf_op jit(solution)/shard_map/all_gather | solution.py:143
  10.2 4.8 %shard_map.67 = bf16[2048,1024]{1,0:T(8,128)(2,1)S(1)} custom-call(bf16[512,26624]{1,0:T(8,128)(2,1)} %base_ref.4), custom_call_target="tpu_custom_call" | custom-call | bytes 8388608 | tf_op jit(solution)/shard_map/pallas_call | solution.py:30
  17.0 4.9 %all-to-all-start.4 = ((bf16[4,512,1024]{2,1,0:T(8,128)(2,1)}), bf16[4,512,1024]{2,1,0:T(8,128)(2,1)}, u32[]{:S(2)}, u32[]{:S(2)}) async-start(bf16[4,512,1024]{2,1,0:T(8,128)(2,1)} %bitcast.14), calls=%async_computation.4 | async-start | bytes 8388608 | tf_op jit(solution)/shard_map/all_to_all | solution.py:149
  21.9 4.8 %shard_map.59 = bf16[2048,1024]{1,0:T(8,128)(2,1)S(1)} custom-call(bf16[512,26624]{1,0:T(8,128)(2,1)} %base_ref.4), custom_call_target="tpu_custom_call" | custom-call | bytes 8388608 | tf_op jit(solution)/shard_map/pallas_call | solution.py:30
  28.7 41.4 %all-to-all-done.4 = bf16[4,512,1024]{2,1,0:T(8,128)(2,1)} async-done(((bf16[4,512,1024]{2,1,0:T(8,128)(2,1)}), bf16[4,512,1024]{2,1,0:T(8,128)(2,1)}, u32[]{:S(2)}, u32[]{:S(2)}) %all-to-all-start.4) | async-done | bytes 4194336 | tf_op jit(solution)/shard_map/all_to_all | solution.py:149
  70.1 4.9 %all-to-all-start = ((bf16[4,512,1024]{2,1,0:T(8,128)(2,1)}), bf16[4,512,1024]{2,1,0:T(8,128)(2,1)}, u32[]{:S(2)}, u32[]{:S(2)}) async-start(bf16[4,512,1024]{2,1,0:T(8,128)(2,1)} %bitcast.13), calls=%async_computation | async-start | bytes 8388608 | tf_op jit(solution)/shard_map/all_to_all | solution.py:149
  75.0 7.1 %shard_map.65 = bf16[2048,1536]{1,0:T(8,128)(2,1)S(1)} custom-call(bf16[512,26624]{1,0:T(8,128)(2,1)} %base_ref.4), custom_call_target="tpu_custom_call" | custom-call | bytes 12582912 | tf_op jit(solution)/shard_map/pallas_call | solution.py:30
  82.2 2.6 copy-done.2
  84.8 38.4 %all-to-all-done = bf16[4,512,1024]{2,1,0:T(8,128)(2,1)} async-done(((bf16[4,512,1024]{2,1,0:T(8,128)(2,1)}), bf16[4,512,1024]{2,1,0:T(8,128)(2,1)}, u32[]{:S(2)}, u32[]{:S(2)}) %all-to-all-start) | async-done | bytes 4194336 | tf_op jit(solution)/shard_map/all_to_all | solution.py:149
  123.2 5.2 %all-to-all-start.3 = ((bf16[4,512,1536]{2,1,0:T(8,128)(2,1)}), bf16[4,512,1536]{2,1,0:T(8,128)(2,1)}, u32[]{:S(2)}, u32[]{:S(2)}) async-start(bf16[4,512,1536]{2,1,0:T(8,128)(2,1)} %bitcast.11), calls=%async_computation.3 | async-start | bytes 12582912 | tf_op jit(solution)/shard_map/all_to_all | solution.py:149
  128.5 7.1 %shard_map.63 = bf16[2048,1536]{1,0:T(8,128)(2,1)S(1)} custom-call(bf16[512,26624]{1,0:T(8,128)(2,1)} %base_ref.4), custom_call_target="tpu_custom_call" | custom-call | bytes 12582912 | tf_op jit(solution)/shard_map/pallas_call | solution.py:30
  135.6 2.7 copy-done.3
  138.3 60.8 %all-to-all-done.3 = bf16[4,512,1536]{2,1,0:T(8,128)(2,1)} async-done(((bf16[4,512,1536]{2,1,0:T(8,128)(2,1)}), bf16[4,512,1536]{2,1,0:T(8,128)(2,1)}, u32[]{:S(2)}, u32[]{:S(2)}) %all-to-all-start.3) | async-done | bytes 6291488 | tf_op jit(solution)/shard_map/all_to_all | solution.py:149
  199.2 5.2 %all-to-all-start.2 = ((bf16[4,512,1536]{2,1,0:T(8,128)(2,1)}), bf16[4,512,1536]{2,1,0:T(8,128)(2,1)}, u32[]{:S(2)}, u32[]{:S(2)}) async-start(bf16[4,512,1536]{2,1,0:T(8,128)(2,1)} %bitcast.12), calls=%async_computation.2 | async-start | bytes 12582912 | tf_op jit(solution)/shard_map/all_to_all | solution.py:149
  204.4 7.2 %shard_map.61 = bf16[2048,1536]{1,0:T(8,128)(2,1)S(1)} custom-call(bf16[512,26624]{1,0:T(8,128)(2,1)} %base_ref.4), custom_call_target="tpu_custom_call" | custom-call | bytes 12582912 | tf_op jit(solution)/shard_map/pallas_call | solution.py:30
  214.2 60.9 %all-to-all-done.2 = bf16[4,512,1536]{2,1,0:T(8,128)(2,1)} async-done(((bf16[4,512,1536]{2,1,0:T(8,128)(2,1)}), bf16[4,512,1536]{2,1,0:T(8,128)(2,1)}, u32[]{:S(2)}, u32[]{:S(2)}) %all-to-all-start.2) | async-done | bytes 6291488 | tf_op jit(solution)/shard_map/all_to_all | solution.py:149
  275.1 5.4 %all-to-all-start.1 = ((bf16[4,512,1536]{2,1,0:T(8,128)(2,1)}), bf16[4,512,1536]{2,1,0:T(8,128)(2,1)}, u32[]{:S(2)}, u32[]{:S(2)}) async-start(bf16[4,512,1536]{2,1,0:T(8,128)(2,1)} %bitcast.10), calls=%async_computation.1 | async-start | bytes 12582912 | tf_op jit(solution)/shard_map/all_to_all | solution.py:149
  281.4 3.0 shard_map.68
  284.5 21.7 %psum.35.squares_ref = f32[1,1024]{1,0:T(1,128)S(1)} all-reduce(f32[1,1024]{1,0:T(1,128)S(1)} %shard_map.68), channel_id=1, replica_groups=mesh['fsdp'=8,'tp'=4] {'fsdp'}, use_global_device_ids=true, to_apply=%region_0.0 | all-reduce | flops 1024 | bytes 8192 | tf_op jit(solution)/shard_map/psum | solution.py:153
  306.2 3.0 shard_map.60
  309.2 5.9 %shard_map.69 = (bf16[2048,6656]{1,0:T(8,128)(2,1)}, f32[16,52]{1,0:T(8,128)}) custom-call(bf16[2048,1024]{1,0:T(8,128)(2,1)} %bitcast.9.piece_ref, bf16[2048,64]{1,0:T(8,128)(2,1)S(1)} %all_gather.3.left_ref, bf16[64,6656]{1,0:T(8,128)(2,1)S(1)} %copy-done, f32[1,1024]{1,0:T(1,128)S(1)} %psum.35.squares_ref, f32[1,6656]{1,0:T(1,128)S(1)} %reshape.17.mag_ref), custom_call_target="tpu_custom_call" | custom-call | flops 268435456 | bytes 8388608 | tf_op jit(solution)/shard_map/pallas_call | solution.py:118
  315.1 4.6 %shard_map.66 = f32[1,1536]{1,0:T(1,128)S(1)} custom-call(bf16[2048,1536]{1,0:T(8,128)(2,1)} %bitcast.7.piece_ref, bf16[2048,64]{1,0:T(8,128)(2,1)S(1)} %all_gather.3.left_ref, bf16[64,6656]{1,0:T(8,128)(2,1)S(1)} %copy-done), custom_call_target="tpu_custom_call" | custom-call | flops 402653184 | bytes 6291456 | tf_op jit(solution)/shard_map/pallas_call | solution.py:58
  319.7 17.4 %psum.36.squares_ref = f32[1,1536]{1,0:T(1,128)S(1)} all-reduce(f32[1,1536]{1,0:T(1,128)S(1)} %shard_map.66), channel_id=1, replica_groups=mesh['fsdp'=8,'tp'=4] {'fsdp'}, use_global_device_ids=true, to_apply=%region_1.0 | all-reduce | flops 1536 | bytes 12288 | tf_op jit(solution)/shard_map/psum | solution.py:153
  337.1 4.6 %shard_map.64 = f32[1,1536]{1,0:T(1,128)S(1)} custom-call(bf16[2048,1536]{1,0:T(8,128)(2,1)} %bitcast.5.piece_ref, bf16[2048,64]{1,0:T(8,128)(2,1)S(1)} %all_gather.3.left_ref, bf16[64,6656]{1,0:T(8,128)(2,1)S(1)} %copy-done), custom_call_target="tpu_custom_call" | custom-call | flops 402653184 | bytes 6291456 | tf_op jit(solution)/shard_map/pallas_call | solution.py:58
  341.7 19.3 %psum.37.squares_ref = f32[1,1536]{1,0:T(1,128)S(1)} all-reduce(f32[1,1536]{1,0:T(1,128)S(1)} %shard_map.64), channel_id=1, replica_groups=mesh['fsdp'=8,'tp'=4] {'fsdp'}, use_global_device_ids=true, to_apply=%region_2.0 | all-reduce | flops 1536 | bytes 12288 | tf_op jit(solution)/shard_map/psum | solution.py:153
  361.1 4.6 %shard_map.62 = f32[1,1536]{1,0:T(1,128)S(1)} custom-call(bf16[2048,1536]{1,0:T(8,128)(2,1)} %bitcast.3.piece_ref, bf16[2048,64]{1,0:T(8,128)(2,1)S(1)} %all_gather.3.left_ref, bf16[64,6656]{1,0:T(8,128)(2,1)S(1)} %copy-done), custom_call_target="tpu_custom_call" | custom-call | flops 402653184 | bytes 6291456 | tf_op jit(solution)/shard_map/pallas_call | solution.py:58
  365.7 17.4 %psum.38.squares_ref = f32[1,1536]{1,0:T(1,128)S(1)} all-reduce(f32[1,1536]{1,0:T(1,128)S(1)} %shard_map.62), channel_id=1, replica_groups=mesh['fsdp'=8,'tp'=4] {'fsdp'}, use_global_device_ids=true, to_apply=%region_3.0 | all-reduce | flops 1536 | bytes 12288 | tf_op jit(solution)/shard_map/psum | solution.py:153
  383.1 19.3 %psum.39.squares_ref = f32[1,1024]{1,0:T(1,128)S(1)} all-reduce(f32[1,1024]{1,0:T(1,128)S(1)} %shard_map.60), channel_id=1, replica_groups=mesh['fsdp'=8,'tp'=4] {'fsdp'}, use_global_device_ids=true, to_apply=%region_4.0 | all-reduce | flops 1024 | bytes 8192 | tf_op jit(solution)/shard_map/psum | solution.py:153
  402.5 8.3 %shard_map.70 = (bf16[2048,6656]{1,0:T(8,128)(2,1)}, f32[16,52]{1,0:T(8,128)}) custom-call(bf16[2048,1536]{1,0:T(8,128)(2,1)} %bitcast.7.piece_ref, bf16[2048,64]{1,0:T(8,128)(2,1)S(1)} %all_gather.3.left_ref, bf16[64,6656]{1,0:T(8,128)(2,1)S(1)} %copy-done, f32[1,1536]{1,0:T(1,128)S(1)} %psum.36.squares_ref, ...), custom_call_target="tpu_custom_call", output_to_operand_aliasing={{0}: (5, {}), {1}: (6, {})} | custom-call | flops 402653184 | bytes 12582912 | tf_op jit(solution)/shard_map/pallas_call | solution.py:118
  410.7 8.2 %shard_map.71 = (bf16[2048,6656]{1,0:T(8,128)(2,1)}, f32[16,52]{1,0:T(8,128)}) custom-call(bf16[2048,1536]{1,0:T(8,128)(2,1)} %bitcast.5.piece_ref, bf16[2048,64]{1,0:T(8,128)(2,1)S(1)} %all_gather.3.left_ref, bf16[64,6656]{1,0:T(8,128)(2,1)S(1)} %copy-done, f32[1,1536]{1,0:T(1,128)S(1)} %psum.37.squares_ref, ...), custom_call_target="tpu_custom_call", output_to_operand_aliasing={{0}: (5, {}), {1}: (6, {})} | custom-call | flops 402653184 | bytes 12582912 | tf_op jit(solution)/shard_map/pallas_call | solution.py:118
  418.9 8.2 %shard_map.72 = (bf16[2048,6656]{1,0:T(8,128)(2,1)}, f32[16,52]{1,0:T(8,128)}) custom-call(bf16[2048,1536]{1,0:T(8,128)(2,1)} %bitcast.3.piece_ref, bf16[2048,64]{1,0:T(8,128)(2,1)S(1)} %all_gather.3.left_ref, bf16[64,6656]{1,0:T(8,128)(2,1)S(1)} %copy-done, f32[1,1536]{1,0:T(1,128)S(1)} %psum.38.squares_ref, ...), custom_call_target="tpu_custom_call", output_to_operand_aliasing={{0}: (5, {}), {1}: (6, {})} | custom-call | flops 402653184 | bytes 12582912 | tf_op jit(solution)/shard_map/pallas_call | solution.py:118
  427.2 5.9 %shard_map.73 = (bf16[2048,6656]{1,0:T(8,128)(2,1)}, f32[16,52]{1,0:T(8,128)}) custom-call(bf16[2048,1024]{1,0:T(8,128)(2,1)} %bitcast.1.piece_ref, bf16[2048,64]{1,0:T(8,128)(2,1)S(1)} %all_gather.3.left_ref, bf16[64,6656]{1,0:T(8,128)(2,1)S(1)} %copy-done, f32[1,1024]{1,0:T(1,128)S(1)} %psum.39.squares_ref, ...), custom_call_target="tpu_custom_call", output_to_operand_aliasing={{0}: (5, {}), {1}: (6, {})} | custom-call | flops 268435456 | bytes 8388608 | tf_op jit(solution)/shard_map/pallas_call | solution.py:118
  (14 shorter events, 8.4 us)
Async XLA Ops:
  15.0 1.9 copy-start.5
  17.0 53.1 %all-to-all-start.4 = ((bf16[4,512,1024]{2,1,0:T(8,128)(2,1)}), bf16[4,512,1024]{2,1,0:T(8,128)(2,1)}, u32[]{:S(2)}, u32[]{:S(2)}) async-start(bf16[4,512,1024]{2,1,0:T(8,128)(2,1)} %bitcast.14), calls=%async_computation.4 | async-start | bytes 8388608 | tf_op jit(solution)/shard_map/all_to_all | solution.py:149
  26.7 2.0 copy-start.4
  70.1 53.1 %all-to-all-start = ((bf16[4,512,1024]{2,1,0:T(8,128)(2,1)}), bf16[4,512,1024]{2,1,0:T(8,128)(2,1)}, u32[]{:S(2)}, u32[]{:S(2)}) async-start(bf16[4,512,1024]{2,1,0:T(8,128)(2,1)} %bitcast.13), calls=%async_computation | async-start | bytes 8388608 | tf_op jit(solution)/shard_map/all_to_all | solution.py:149
  82.1 2.6 copy-start.2
  123.2 76.0 %all-to-all-start.3 = ((bf16[4,512,1536]{2,1,0:T(8,128)(2,1)}), bf16[4,512,1536]{2,1,0:T(8,128)(2,1)}, u32[]{:S(2)}, u32[]{:S(2)}) async-start(bf16[4,512,1536]{2,1,0:T(8,128)(2,1)} %bitcast.11), calls=%async_computation.3 | async-start | bytes 12582912 | tf_op jit(solution)/shard_map/all_to_all | solution.py:149
  135.6 2.7 copy-start.3
  199.2 75.9 %all-to-all-start.2 = ((bf16[4,512,1536]{2,1,0:T(8,128)(2,1)}), bf16[4,512,1536]{2,1,0:T(8,128)(2,1)}, u32[]{:S(2)}, u32[]{:S(2)}) async-start(bf16[4,512,1536]{2,1,0:T(8,128)(2,1)} %bitcast.12), calls=%async_computation.2 | async-start | bytes 12582912 | tf_op jit(solution)/shard_map/all_to_all | solution.py:149
  211.6 2.6 copy-start.1
  275.1 6.3 %copy-start = (bf16[64,6656]{1,0:T(8,128)(2,1)S(1)}, bf16[64,6656]{1,0:T(8,128)(2,1)}, u32[]{:S(2)}) copy-start(bf16[64,6656]{1,0:T(8,128)(2,1)} %right_ref.19) | copy-start | bytes 2555908
  275.1 86.0 %all-to-all-start.1 = ((bf16[4,512,1536]{2,1,0:T(8,128)(2,1)}), bf16[4,512,1536]{2,1,0:T(8,128)(2,1)}, u32[]{:S(2)}, u32[]{:S(2)}) async-start(bf16[4,512,1536]{2,1,0:T(8,128)(2,1)} %bitcast.10), calls=%async_computation.1 | async-start | bytes 12582912 | tf_op jit(solution)/shard_map/all_to_all | solution.py:149

commit v2 on v0

v2 whole, which is shorter than its diff:
```python
import functools

import jax
import jax.numpy as jnp
from jax import lax
from jax.experimental import pallas as pl
from jax.experimental.pallas import tpu as pltpu
from jax.sharding import PartitionSpec as P

BLOCK = 128
EPSILON = 1e-06
PARTS = (1, 2, 2, 2, 2, 2, 1, 1)
LATE = 2
AHEAD = 2
PARAMS = pltpu.CompilerParams(vmem_limit_bytes=56 * 2**20)


def chunk_units(total, parts):
    bounds = [0]
    whole = sum(parts)
    for i in range(len(parts)):
        bounds.append(round(total * sum(parts[: i + 1]) / whole))
    return [(a, b) for a, b in zip(bounds, bounds[1:]) if b > a]


def after(value, *others):
    return lax.optimization_barrier((value, *others))[0]


def exchange(arrays, tp):
    return [
        lax.ppermute(array, "tp", [(i, i ^ d) for i in range(tp)])
        for d, array in zip(range(1, tp), arrays)
    ]


def copy_kernel(me_ref, *refs):
    half = len(refs) // 2
    for source, target in zip(refs[:half], refs[half:]):
        target[...] = source[...]


def pack(me, base, tp, unit, first, count):
    rows = base.shape[0]
    group = base.shape[1] // (tp * unit)

    def source(d):
        return pl.BlockSpec((rows, unit), lambda j, me: (0, (me[0] ^ d) * group + first + j))

    return pl.pallas_call(
        copy_kernel,
        out_shape=[jax.ShapeDtypeStruct((rows, count * unit), base.dtype)] * (tp - 1),
        grid_spec=pltpu.PrefetchScalarGridSpec(
            num_scalar_prefetch=1,
            grid=(count,),
            in_specs=[source(d) for d in range(1, tp)],
            out_specs=[pl.BlockSpec((rows, unit), lambda j, me: (0, j))] * (tp - 1),
        ),
        compiler_params=PARAMS,
        cost_estimate=pl.CostEstimate(
            flops=0, bytes_accessed=4 * (tp - 1) * rows * count * unit, transcendentals=0
        ),
    )(me, *[base] * (tp - 1))


def squares_of(piece_ref, left_ref, right_ref):
    rows, cols = piece_ref.shape
    step = min(rows, BLOCK)
    total = jnp.zeros((8, cols), jnp.float32)
    for r in range(0, rows, step):
        span = pl.ds(r, step)
        low_rank = jnp.dot(left_ref[span, :], right_ref[...], preferred_element_type=jnp.float32)
        combined = piece_ref[span, :].astype(jnp.float32) + low_rank
        total = total + jnp.sum((combined * combined).reshape(step // 8, 8, cols), axis=0)
    return total


def squares_kernel(tp, me_ref, *refs):
    pieces, lefts, right_ref, out_ref = refs[:tp], refs[tp : 2 * tp], refs[-2], refs[-1]
    total = sum(squares_of(piece, left, right_ref) for piece, left in zip(pieces, lefts))
    out_ref[...] = jnp.sum(total, axis=0, keepdims=True)


def sender_squares_kernel(tp, me_ref, *refs):
    pieces, left_ref, rights, outs = refs[:tp], refs[tp], refs[tp + 1 : 2 * tp + 1], refs[2 * tp + 1 :]
    for piece, right, out_ref in zip(pieces, rights, outs):
        out_ref[...] = jnp.sum(squares_of(piece, left_ref, right), axis=0, keepdims=True)


def own_spec(rows, unit, group, first):
    return pl.BlockSpec((rows, unit), lambda j, me: (0, me[0] * group + first + j))


def whole_spec(array):
    return pl.BlockSpec(array.shape, lambda j, me: (0, 0))


def chunk_spec(rows, unit):
    return pl.BlockSpec((rows, unit), lambda j, me: (0, j))


def matmul_cost(rows, cols, rank, passes):
    return pl.CostEstimate(
        flops=2 * rows * cols * rank, bytes_accessed=2 * passes * rows * cols, transcendentals=0
    )


def column_squares(me, base, received, lefts, right, unit, first, count):
    rows, rank = lefts[0].shape
    tp = len(lefts)
    group = right.shape[1] // unit
    return pl.pallas_call(
        functools.partial(squares_kernel, tp),
        out_shape=jax.ShapeDtypeStruct((1, count * unit), jnp.float32),
        grid_spec=pltpu.PrefetchScalarGridSpec(
            num_scalar_prefetch=1,
            grid=(count,),
            in_specs=[own_spec(rows, unit, group, first)]
            + [chunk_spec(rows, unit)] * (tp - 1)
            + [whole_spec(left) for left in lefts]
            + [pl.BlockSpec((rank, unit), lambda j, me: (0, first + j))],
            out_specs=chunk_spec(1, unit),
        ),
        compiler_params=PARAMS,
        cost_estimate=matmul_cost(tp * rows, count * unit, rank, 1),
    )(me, base, *received, *lefts, right)


def sender_squares(me, base, packed, left, right, rights, unit, first, count):
    rows, rank = left.shape
    tp = len(packed) + 1
    group = right.shape[1] // unit
    return pl.pallas_call(
        functools.partial(sender_squares_kernel, tp),
        out_shape=[jax.ShapeDtypeStruct((1, count * unit), jnp.float32)] * tp,
        grid_spec=pltpu.PrefetchScalarGridSpec(
            num_scalar_prefetch=1,
            grid=(count,),
            in_specs=[own_spec(rows, unit, group, first)]
            + [chunk_spec(rows, unit)] * (tp - 1)
            + [whole_spec(left), pl.BlockSpec((rank, unit), lambda j, me: (0, first + j))]
            + [chunk_spec(rank, unit)] * (tp - 1),
            out_specs=[chunk_spec(1, unit)] * tp,
        ),
        compiler_params=PARAMS,
        cost_estimate=matmul_cost(tp * rows, count * unit, rank, 1),
    )(me, base, *packed, left, right, *rights)


def export_kernel(tp, first, me_ref, *refs):
    pieces, lefts = refs[:tp], refs[tp : 2 * tp]
    right_ref, squares_ref, mag_ref = refs[2 * tp : 2 * tp + 3]
    out_ref, scales_ref = refs[-2:]
    rows, cols = pieces[0].shape
    step = pl.program_id(0)
    if len(refs) > 2 * tp + 5:
        @pl.when(step == 0)
        def _():
            scales_ref[...] = refs[2 * tp + 4][...]

    factor = mag_ref[...] / jnp.sqrt(squares_ref[...] + EPSILON)
    height = min(rows, BLOCK)
    for d in range(tp):
        start = (me_ref[0] ^ d) * rows
        for r in range(0, rows, height):
            low_rank = jnp.dot(lefts[d][pl.ds(r, height), :], right_ref[...], preferred_element_type=jnp.float32)
            combined = pieces[d][pl.ds(r, height), :].astype(jnp.float32) + low_rank
            span = pl.ds(pl.multiple_of(start + r, height), height)
            out_ref[span, :] = (combined * factor).astype(jnp.bfloat16)

    lane = lax.broadcasted_iota(jnp.int32, (1, scales_ref.shape[1]), 1)
    per_step = cols // BLOCK
    for i in range(tp * rows // BLOCK):
        span = pl.ds(i * BLOCK, BLOCK)
        line = scales_ref[pl.ds(i, 1), :]
        for j in range(per_step):
            tile = out_ref[span, pl.ds(j * BLOCK, BLOCK)].astype(jnp.float32)
            largest = jnp.max(jnp.max(jnp.abs(tile), axis=0, keepdims=True), axis=1, keepdims=True)
            out_ref[span, pl.ds(j * BLOCK, BLOCK)] = (tile * (1.0 / (largest + EPSILON))).astype(jnp.bfloat16)
            line = jnp.where(lane == (first + step) * per_step + j, largest, line)
        scales_ref[pl.ds(i, 1), :] = line


def export_chunk(me, base, received, lefts, right, squares, mag, unit, first, count, previous):
    rows, rank = lefts[0].shape
    tp = len(lefts)
    all_cols = right.shape[1]
    group = all_cols // unit
    result = (
        jax.ShapeDtypeStruct((tp * rows, all_cols), jnp.bfloat16),
        jax.ShapeDtypeStruct((tp * rows // BLOCK, all_cols // BLOCK), jnp.float32),
    )
    in_specs = (
        [own_spec(rows, unit, group, first)]
        + [chunk_spec(rows, unit)] * (tp - 1)
        + [whole_spec(left) for left in lefts]
        + [
            pl.BlockSpec((rank, unit), lambda j, me: (0, first + j)),
            chunk_spec(1, unit),
            own_spec(1, unit, group, first),
        ]
    )
    args = [base, *received, *lefts, right, squares, mag]
    aliases = {}
    if previous is not None:
        in_specs += [pl.BlockSpec(memory_space=pl.ANY), whole_spec(previous[1])]
        args += list(previous)
        aliases = {len(args) - 1: 0}
    return pl.pallas_call(
        functools.partial(export_kernel, tp, first),
        out_shape=result,
        grid_spec=pltpu.PrefetchScalarGridSpec(
            num_scalar_prefetch=1,
            grid=(count,),
            in_specs=in_specs,
            out_specs=(pl.BlockSpec((tp * rows, unit), lambda j, me: (0, first + j)), whole_spec(result[1])),
        ),
        input_output_aliases=aliases,
        compiler_params=PARAMS,
        cost_estimate=matmul_cost(tp * rows, count * unit, rank, 2),
    )(me, *args)


def body(tp, base, left, right, magnitude):
    cols = right.shape[1]
    blocks = cols // BLOCK
    unit = max(d for d in (4, 2, 1) if blocks % d == 0) * BLOCK
    chunks = chunk_units(cols // unit, PARTS)
    mag = magnitude.reshape(1, -1)
    me = lax.axis_index("tp").astype(jnp.int32).reshape(1)
    early = len(chunks) - LATE

    lefts = [left] + exchange([left] * (tp - 1), tp)

    def send(k, me):
        a, b = chunks[k]
        return exchange(pack(me, base, tp, unit, a, b - a), tp)

    received = {}
    for k in range(AHEAD):
        received[k] = send(k, me)

    totals = {}
    packed = {}
    begin = after(me, received[0][0])
    for k in range(early, len(chunks)):
        a, b = chunks[k]
        packed[k] = pack(begin, base, tp, unit, a, b - a)
        rights = exchange([right[:, a * unit : b * unit]] * (tp - 1), tp)
        sums = sender_squares(begin, base, packed[k], left, right, rights, unit, a, b - a)
        totals[k] = sum(exchange(sums[1:], tp), sums[0])
    last = ()

    result = None
    scales = []
    for k in range(len(chunks)):
        a, b = chunks[k]
        following = k + AHEAD
        if following < len(chunks):
            done = list(received[k])
            if scales:
                done.append(scales[-1])
            done += last
            if following < early:
                received[following] = send(following, after(me, *done))
            else:
                sent = lax.optimization_barrier((*packed[following], *done))[: tp - 1]
                received[following] = exchange(sent, tp)
        if k < early:
            local = column_squares(me, base, received[k], lefts, right, unit, a, b - a)
            totals[k] = lax.psum(after(local, *last), "fsdp")
            last = (totals[k],)
        if k == 0:
            held = [after(totals[i], *last) for i in range(early, len(chunks))]
            last = lax.psum(tuple(held), "fsdp")
            totals.update({early + i: total for i, total in enumerate(last)})
        result = export_chunk(me, base, received[k], lefts, right, totals[k], mag, unit, a, b - a, result)
        scales.append(result[1])
    return result


def solution(mesh):
    in_specs = (P(("fsdp", "tp"), None), P(("fsdp", "tp"), None), P(None, "tp"), P())
    out_specs = (P("fsdp", "tp"), P("fsdp", "tp"))
    return jax.shard_map(
        functools.partial(body, mesh.shape["tp"]), mesh=mesh, in_specs=in_specs, out_specs=out_specs, check_vma=False
    )
```

time: 658 us -> 362 us (0.55)
  blocking collectives: 336 us -> 135 us
  local copies, waits for them, and re-layouts: 184 us -> 1.99 us
  Pallas kernels: 0 us -> 98.8 us
  other arithmetic: 98.5 us -> 0.02 us
  waiting for transfers between devices: 0.01 us -> 95.5 us
  matrix products: 27.3 us -> 0 us
  starting transfers between devices: 8.74 us -> 27.9 us
    all_gather x1 -> x0, blocking collectives: 297 us -> none  [body(): lax.all_gather(left_factor, 'tp', axis=0, tiled=True)]
    pallas_call x0 -> x24, Pallas kernels: none -> 98.8 us  [the longest x8 45.2 us: export_chunk(): pl.pallas_call(functools.partial(export_kernel, tp, first), out_shape=res...]
    psum x1 -> x7, blocking collectives: 38.2 us -> 135 us  [the longest x6 118 us: body(): totals[k] = lax.psum(after(local, *last), 'fsdp')]
    ppermute x0 -> x39, waiting for transfers between devices: none -> 95.5 us  [exchange(): lax.ppermute(array, 'tp', [(i, i ^ d) for i in range(tp)])]
    div x2 -> x0, local copies, waits for them, and re-layouts: 67.7 us -> none  [to_blocks(): scaled = tile_view / (block_max[:, None, :, None] + epsilon)]
    abs x1 -> x0, local copies, waits for them, and re-layouts: 58.7 us -> none  [to_blocks(): block_max = jnp.max(jnp.abs(tile_view), axis=(1, 3))]
    convert_element_type x1 -> x0, other arithmetic: 44.2 us -> none  [to_blocks(): scaled.astype(jnp.bfloat16).reshape(row_count, col_count)]
    unnamed x10 -> x59, local copies, waits for them, and re-layouts: 37.7 us -> 1.11 us
  transfers between devices with their start and end apart: 1 -> 39, of which waited for: 0 -> 13; matrix products, arithmetic and copies ran while one was open for 0% -> 0% of each run, Pallas kernels for 0% -> 25%
where the time goes in v2:
time: 362 us; the launch traced here: 361 us
  blocking collectives  135 us (37%)
  Pallas kernels  98.8 us (27%)
  waiting for transfers between devices  95.5 us (26%)
  starting transfers between devices  27.9 us (8%)
    psum x6, blocking collectives, body(): totals[k] = lax.psum(after(local, *last), 'fsdp')  118 us
    ppermute x39, waiting for transfers between devices, exchange(): lax.ppermute(array, 'tp', [(i, i ^ d) for i in range(tp)])  95.5 us
    pallas_call x8, Pallas kernels, export_chunk(): pl.pallas_call(functools.partial(export_kernel, tp, first), out_shape=res...  45.2 us
    ppermute x39, starting transfers between devices, exchange(): lax.ppermute(array, 'tp', [(i, i ^ d) for i in range(tp)])  27.9 us
    pallas_call x8, Pallas kernels, pack(): pl.pallas_call(copy_kernel, out_shape=[jax.ShapeDtypeStruct((rows, count...  24 us
    pallas_call x6, Pallas kernels, column_squares(): pl.pallas_call(functools.partial(squares_kernel, tp), out_shape=jax.Shape...  23.8 us
    psum x1, blocking collectives, body(): last = lax.psum(tuple(held), 'fsdp')  17.7 us
  transfers between devices with their start and end apart: 39, of which 13 were waited for; matrix products, arithmetic and copies ran while one was open for 0% of the time, Pallas kernels for 25%

profile of v2, /device:TPU:0, one launch (start us, length us, event | category | flops | bytes accessed | tf_op | source)
XLA Modules:
  0.0 360.7 jit_solution(319299392095922454)
XLA Ops:
  0.6 3.2 shard_map.61
  21.2 24.4 %collective-permute-done.8.refs_7_ = bf16[512,64]{1,0:T(8,128)(2,1)S(1)} collective-permute-done((bf16[512,64]{1,0:T(8,128)(2,1)S(1)}, bf16[512,64]{1,0:T(8,128)(2,1)S(1)}, u32[]{:S(2)}, u32[]{:S(2)}) %collective-permute-start.8) | collective-permute-done | bytes 65568 | tf_op jit(solution)/shard_map/ppermute | solution.py:32
  51.7 3.2 shard_map.68
  55.0 41.3 %collective-permute-done.7.refs_6_ = bf16[512,64]{1,0:T(8,128)(2,1)S(1)} collective-permute-done((bf16[512,64]{1,0:T(8,128)(2,1)S(1)}, bf16[512,64]{1,0:T(8,128)(2,1)S(1)}, u32[]{:S(2)}, u32[]{:S(2)}) %collective-permute-start.7) | collective-permute-done | bytes 65568 | tf_op jit(solution)/shard_map/ppermute | solution.py:32
  96.2 3.0 shard_map.65
  114.2 3.2 collective-permute-done.20
  118.4 3.2 shard_map.62
  121.7 22.4 %psum.56.refs_9_ = f32[1,512]{1,0:T(1,128)} all-reduce(f32[1,512]{1,0:T(1,128)} %shard_map.62), channel_id=1, replica_groups=mesh['fsdp'=8,'tp'=4] {'fsdp'}, use_global_device_ids=true, to_apply=%region_0.0 | all-reduce | flops 512 | bytes 4096 | tf_op jit(solution)/shard_map/psum | solution.py:271
  144.0 4.4 %shard_map.63 = (bf16[2048,6656]{1,0:T(8,128)(2,1)}, f32[16,52]{1,0:T(8,128)}) custom-call(s32[1]{0:T(128)} %bitcast.me_ref, bf16[512,26624]{1,0:T(8,128)(2,1)} %refs_0_.47, bf16[512,512]{1,0:T(8,128)(2,1)} %copy-done.10, bf16[512,512]{1,0:T(8,128)(2,1)} %copy-done.11, bf16[512,512]{1,0:T(8,128)(2,1)} %copy-done.12, bf16[512,64]{1,0:T(8,128)(2,1)} %copy-done, ...), custom_call_target="tpu_custom_call" | custom-call | flops 134217728 | bytes 4194304 | tf_op jit(solution)/shard_map/pallas_call | solution.py:209
  148.5 17.7 %all-reduce = (f32[1,512]{1,0:T(1,128)}, f32[1,512]{1,0:T(1,128)}) all-reduce(f32[1,512]{1,0:T(1,128)S(1)} %add_add_fusion.1, f32[1,512]{1,0:T(1,128)S(1)} %add_add_fusion), channel_id=1, replica_groups=mesh['fsdp'=8,'tp'=4] {'fsdp'}, use_global_device_ids=true, to_apply=%region_1.0 | all-reduce | flops 1024 | bytes 8192 | tf_op jit(solution)/shard_map/psum | solution.py:275
  166.2 3.3 shard_map.67
  169.5 4.1 %shard_map.70 = f32[1,1024]{1,0:T(1,128)} custom-call(s32[1]{0:T(128)} %bitcast.me_ref, bf16[512,26624]{1,0:T(8,128)(2,1)} %refs_0_.47, bf16[512,1024]{1,0:T(8,128)(2,1)} %copy-done.4, bf16[512,1024]{1,0:T(8,128)(2,1)} %collective-permute-done.2.refs_2_, bf16[512,1024]{1,0:T(8,128)(2,1)} %collective-permute-done.3.refs_3_, bf16[512,64]{1,0:T(8,128)(2,1)} %copy-done, ...), custom_call_target="tpu_custom_call" | custom-call | flops 268435456 | bytes 4194304 | tf_op jit(solution)/shard_map/pallas_call | solution.py:112
  174.7 19.8 %psum.59.refs_9_ = f32[1,1024]{1,0:T(1,128)} all-reduce(f32[1,1024]{1,0:T(1,128)} %shard_map.70), channel_id=1, replica_groups=mesh['fsdp'=8,'tp'=4] {'fsdp'}, use_global_device_ids=true, to_apply=%region_3.0 | all-reduce | flops 1024 | bytes 8192 | tf_op jit(solution)/shard_map/psum | solution.py:271
  194.5 6.6 %shard_map.71 = (bf16[2048,6656]{1,0:T(8,128)(2,1)}, f32[16,52]{1,0:T(8,128)}) custom-call(s32[1]{0:T(128)} %bitcast.me_ref, bf16[512,26624]{1,0:T(8,128)(2,1)} %refs_0_.47, bf16[512,1024]{1,0:T(8,128)(2,1)} %copy-done.4, bf16[512,1024]{1,0:T(8,128)(2,1)} %collective-permute-done.2.refs_2_, ...), custom_call_target="tpu_custom_call", output_to_operand_aliasing={{0}: (12, {})} | custom-call | flops 268435456 | bytes 8388608 | tf_op jit(solution)/shard_map/pallas_call | solution.py:209
  201.2 3.2 shard_map.74
  206.4 4.3 %shard_map.69 = f32[1,1024]{1,0:T(1,128)} custom-call(s32[1]{0:T(128)} %bitcast.me_ref, bf16[512,26624]{1,0:T(8,128)(2,1)} %refs_0_.47, bf16[512,1024]{1,0:T(8,128)(2,1)} %copy-done.5, bf16[512,1024]{1,0:T(8,128)(2,1)} %collective-permute-done.25.refs_2_, bf16[512,1024]{1,0:T(8,128)(2,1)} %collective-permute-done.26.refs_3_, bf16[512,64]{1,0:T(8,128)(2,1)} %copy-done, ...), custom_call_target="tpu_custom_call" | custom-call | flops 268435456 | bytes 4194304 | tf_op jit(solution)/shard_map/pallas_call | solution.py:112
  210.7 18.0 %psum.60.refs_9_ = f32[1,1024]{1,0:T(1,128)} all-reduce(f32[1,1024]{1,0:T(1,128)} %shard_map.69), channel_id=1, replica_groups=mesh['fsdp'=8,'tp'=4] {'fsdp'}, use_global_device_ids=true, to_apply=%region_4.0 | all-reduce | flops 1024 | bytes 8192 | tf_op jit(solution)/shard_map/psum | solution.py:271
  228.7 6.2 %shard_map.72 = (bf16[2048,6656]{1,0:T(8,128)(2,1)}, f32[16,52]{1,0:T(8,128)}) custom-call(s32[1]{0:T(128)} %bitcast.me_ref, bf16[512,26624]{1,0:T(8,128)(2,1)} %refs_0_.47, bf16[512,1024]{1,0:T(8,128)(2,1)} %copy-done.5, bf16[512,1024]{1,0:T(8,128)(2,1)} %collective-permute-done.25.refs_2_, ...), custom_call_target="tpu_custom_call", output_to_operand_aliasing={{0}: (12, {})} | custom-call | flops 268435456 | bytes 8388608 | tf_op jit(solution)/shard_map/pallas_call | solution.py:209
  235.0 3.3 shard_map.73
  240.2 4.1 %shard_map.76 = f32[1,1024]{1,0:T(1,128)} custom-call(s32[1]{0:T(128)} %bitcast.me_ref, bf16[512,26624]{1,0:T(8,128)(2,1)} %refs_0_.47, bf16[512,1024]{1,0:T(8,128)(2,1)} %copy-done.6, bf16[512,1024]{1,0:T(8,128)(2,1)} %collective-permute-done.22.refs_2_, bf16[512,1024]{1,0:T(8,128)(2,1)} %collective-permute-done.23.refs_3_, bf16[512,64]{1,0:T(8,128)(2,1)} %copy-done, ...), custom_call_target="tpu_custom_call" | custom-call | flops 268435456 | bytes 4194304 | tf_op jit(solution)/shard_map/pallas_call | solution.py:112
  244.3 19.7 %psum.61.refs_9_ = f32[1,1024]{1,0:T(1,128)} all-reduce(f32[1,1024]{1,0:T(1,128)} %shard_map.76), channel_id=1, replica_groups=mesh['fsdp'=8,'tp'=4] {'fsdp'}, use_global_device_ids=true, to_apply=%region_5.0 | all-reduce | flops 1024 | bytes 8192 | tf_op jit(solution)/shard_map/psum | solution.py:271
  264.0 6.3 %shard_map.77 = (bf16[2048,6656]{1,0:T(8,128)(2,1)}, f32[16,52]{1,0:T(8,128)}) custom-call(s32[1]{0:T(128)} %bitcast.me_ref, bf16[512,26624]{1,0:T(8,128)(2,1)} %refs_0_.47, bf16[512,1024]{1,0:T(8,128)(2,1)} %copy-done.6, bf16[512,1024]{1,0:T(8,128)(2,1)} %collective-permute-done.22.refs_2_, ...), custom_call_target="tpu_custom_call", output_to_operand_aliasing={{0}: (12, {})} | custom-call | flops 268435456 | bytes 8388608 | tf_op jit(solution)/shard_map/pallas_call | solution.py:209
  271.3 4.0 %shard_map.75 = f32[1,1024]{1,0:T(1,128)} custom-call(s32[1]{0:T(128)} %bitcast.me_ref, bf16[512,26624]{1,0:T(8,128)(2,1)} %refs_0_.47, bf16[512,1024]{1,0:T(8,128)(2,1)} %copy-done.7, bf16[512,1024]{1,0:T(8,128)(2,1)} %copy-done.8, bf16[512,1024]{1,0:T(8,128)(2,1)} %collective-permute-done.32.refs_3_, bf16[512,64]{1,0:T(8,128)(2,1)} %copy-done, ...), custom_call_target="tpu_custom_call" | custom-call | flops 268435456 | bytes 4194304 | tf_op jit(solution)/shard_map/pallas_call | solution.py:112
  276.2 17.8 %psum.62.refs_9_ = f32[1,1024]{1,0:T(1,128)} all-reduce(f32[1,1024]{1,0:T(1,128)} %shard_map.75), channel_id=1, replica_groups=mesh['fsdp'=8,'tp'=4] {'fsdp'}, use_global_device_ids=true, to_apply=%region_6.0 | all-reduce | flops 1024 | bytes 8192 | tf_op jit(solution)/shard_map/psum | solution.py:271
  294.1 6.7 %shard_map.78 = (bf16[2048,6656]{1,0:T(8,128)(2,1)}, f32[16,52]{1,0:T(8,128)}) custom-call(s32[1]{0:T(128)} %bitcast.me_ref, bf16[512,26624]{1,0:T(8,128)(2,1)} %refs_0_.47, bf16[512,1024]{1,0:T(8,128)(2,1)} %copy-done.7, bf16[512,1024]{1,0:T(8,128)(2,1)} %copy-done.8, ...), custom_call_target="tpu_custom_call", output_to_operand_aliasing={{0}: (12, {})} | custom-call | flops 268435456 | bytes 8388608 | tf_op jit(solution)/shard_map/pallas_call | solution.py:209
  300.8 10.5 %collective-permute-done.29.refs_3_ = bf16[512,1024]{1,0:T(8,128)(2,1)} collective-permute-done((bf16[512,1024]{1,0:T(8,128)(2,1)}, bf16[512,1024]{1,0:T(8,128)(2,1)}, u32[]{:S(2)}, u32[]{:S(2)}) %collective-permute-start.29) | collective-permute-done | bytes 1048608 | tf_op jit(solution)/shard_map/ppermute | solution.py:32
  313.5 4.0 %shard_map.79 = f32[1,1024]{1,0:T(1,128)} custom-call(s32[1]{0:T(128)} %bitcast.me_ref, bf16[512,26624]{1,0:T(8,128)(2,1)} %refs_0_.47, bf16[512,1024]{1,0:T(8,128)(2,1)} %copy-done.9, bf16[512,1024]{1,0:T(8,128)(2,1)} %collective-permute-done.28.refs_2_, bf16[512,1024]{1,0:T(8,128)(2,1)} %collective-permute-done.29.refs_3_, bf16[512,64]{1,0:T(8,128)(2,1)} %copy-done, ...), custom_call_target="tpu_custom_call" | custom-call | flops 268435456 | bytes 4194304 | tf_op jit(solution)/shard_map/pallas_call | solution.py:112
  317.5 20.0 %psum.63.refs_9_ = f32[1,1024]{1,0:T(1,128)} all-reduce(f32[1,1024]{1,0:T(1,128)} %shard_map.79), channel_id=1, replica_groups=mesh['fsdp'=8,'tp'=4] {'fsdp'}, use_global_device_ids=true, to_apply=%region_7.0 | all-reduce | flops 1024 | bytes 8192 | tf_op jit(solution)/shard_map/psum | solution.py:271
  337.5 6.2 %shard_map.80 = (bf16[2048,6656]{1,0:T(8,128)(2,1)}, f32[16,52]{1,0:T(8,128)}) custom-call(s32[1]{0:T(128)} %bitcast.me_ref, bf16[512,26624]{1,0:T(8,128)(2,1)} %refs_0_.47, bf16[512,1024]{1,0:T(8,128)(2,1)} %copy-done.9, bf16[512,1024]{1,0:T(8,128)(2,1)} %collective-permute-done.28.refs_2_, ...), custom_call_target="tpu_custom_call", output_to_operand_aliasing={{0}: (12, {})} | custom-call | flops 268435456 | bytes 8388608 | tf_op jit(solution)/shard_map/pallas_call | solution.py:209
  343.7 4.4 %shard_map.81 = (bf16[2048,6656]{1,0:T(8,128)(2,1)}, f32[16,52]{1,0:T(8,128)}) custom-call(s32[1]{0:T(128)} %bitcast.me_ref, bf16[512,26624]{1,0:T(8,128)(2,1)} %refs_0_.47, bf16[512,512]{1,0:T(8,128)(2,1)} %collective-permute-done.36.refs_1_, bf16[512,512]{1,0:T(8,128)(2,1)} %collective-permute-done.37.refs_2_, ...), custom_call_target="tpu_custom_call", output_to_operand_aliasing={{0}: (12, {})} | custom-call | flops 134217728 | bytes 4194304 | tf_op jit(solution)/shard_map/pallas_call | solution.py:209
  348.2 8.1 %collective-permute-done.35.refs_3_ = bf16[512,512]{1,0:T(8,128)(2,1)} collective-permute-done((bf16[512,512]{1,0:T(8,128)(2,1)S(1)}, bf16[512,512]{1,0:T(8,128)(2,1)}, u32[]{:S(2)}, u32[]{:S(2)}) %collective-permute-start.35) | collective-permute-done | bytes 524320 | tf_op jit(solution)/shard_map/ppermute | solution.py:32
  356.3 4.4 %shard_map.82 = (bf16[2048,6656]{1,0:T(8,128)(2,1)}, f32[16,52]{1,0:T(8,128)}) custom-call(s32[1]{0:T(128)} %bitcast.me_ref, bf16[512,26624]{1,0:T(8,128)(2,1)} %refs_0_.47, bf16[512,512]{1,0:T(8,128)(2,1)} %copy-done.17, bf16[512,512]{1,0:T(8,128)(2,1)} %copy-done.18, ...), custom_call_target="tpu_custom_call", output_to_operand_aliasing={{0}: (12, {})} | custom-call | flops 134217728 | bytes 4194304 | tf_op jit(solution)/shard_map/pallas_call | solution.py:209
  (139 shorter events, 48.4 us)
Async XLA Ops:
  3.8 114.5 %collective-permute-start.1 = (bf16[512,1024]{1,0:T(8,128)(2,1)}, bf16[512,1024]{1,0:T(8,128)(2,1)S(1)}, u32[]{:S(2)}, u32[]{:S(2)}) collective-permute-start(bf16[512,1024]{1,0:T(8,128)(2,1)} %get-tuple-element.71), channel_id=1, source_target_pairs={{0,1},{1,0},{2,3},{3,2},{4,5},{5,4},{6,7},{7,6},{8,9},{9,8},{10,11... | collective-permute-start | bytes 3145736 | tf_op jit(solution)/shard_map/ppermute | solution.py:32
  6.9 40.3 %collective-permute-start = (bf16[512,512]{1,0:T(8,128)(2,1)}, bf16[512,512]{1,0:T(8,128)(2,1)S(1)}, u32[]{:S(2)}, u32[]{:S(2)}) collective-permute-start(bf16[512,512]{1,0:T(8,128)(2,1)} %get-tuple-element.66), channel_id=1, source_target_pairs={{0,1},{1,0},{2,3},{3,2},{4,5},{5,4},{6,7},{7,6},{8,9},{9,8},{10,11... | collective-permute-start | bytes 1572872 | tf_op jit(solution)/shard_map/ppermute | solution.py:32
  7.8 5.1 %collective-permute-start.17 = (bf16[64,512]{1,0:T(8,128)(2,1)S(1)}, bf16[64,512]{1,0:T(8,128)(2,1)S(1)}, u32[]{:S(2)}, u32[]{:S(2)}) collective-permute-start(bf16[64,512]{1,0:T(8,128)(2,1)S(1)} %get-tuple-element.132), channel_id=1, source_target_pairs={{0,3},{1,2},{2,1},{3,0},{4,7},{5,6},{6,5},{7,4},{8,11},{9,10},{10,... | collective-permute-start | bytes 196616 | tf_op jit(solution)/shard_map/ppermute | solution.py:32
  10.5 4.5 %collective-permute-start.16 = (bf16[64,512]{1,0:T(8,128)(2,1)S(1)}, bf16[64,512]{1,0:T(8,128)(2,1)S(1)}, u32[]{:S(2)}, u32[]{:S(2)}) collective-permute-start(bf16[64,512]{1,0:T(8,128)(2,1)S(1)} %get-tuple-element.132), channel_id=1, source_target_pairs={{0,2},{1,3},{2,0},{3,1},{4,6},{5,7},{6,4},{7,5},{8,10},{9,11},{10,... | collective-permute-start | bytes 196616 | tf_op jit(solution)/shard_map/ppermute | solution.py:32
  10.9 5.7 %collective-permute-start.15 = (bf16[64,512]{1,0:T(8,128)(2,1)S(1)}, bf16[64,512]{1,0:T(8,128)(2,1)S(1)}, u32[]{:S(2)}, u32[]{:S(2)}) collective-permute-start(bf16[64,512]{1,0:T(8,128)(2,1)S(1)} %get-tuple-element.132), channel_id=1, source_target_pairs={{0,1},{1,0},{2,3},{3,2},{4,5},{5,4},{6,7},{7,6},{8,9},{9,8},{10,11... | collective-permute-start | bytes 196616 | tf_op jit(solution)/shard_map/ppermute | solution.py:32
  12.9 4.3 %collective-permute-start.11 = (bf16[64,512]{1,0:T(8,128)(2,1)S(1)}, bf16[64,512]{1,0:T(8,128)(2,1)S(1)}, u32[]{:S(2)}, u32[]{:S(2)}) collective-permute-start(bf16[64,512]{1,0:T(8,128)(2,1)S(1)} %get-tuple-element.133), channel_id=1, source_target_pairs={{0,3},{1,2},{2,1},{3,0},{4,7},{5,6},{6,5},{7,4},{8,11},{9,10},{10,... | collective-permute-start | bytes 196616 | tf_op jit(solution)/shard_map/ppermute | solution.py:32
  17.2 30.0 %collective-permute-start.4 = (bf16[512,512]{1,0:T(8,128)(2,1)}, bf16[512,512]{1,0:T(8,128)(2,1)S(1)}, u32[]{:S(2)}, u32[]{:S(2)}) collective-permute-start(bf16[512,512]{1,0:T(8,128)(2,1)} %get-tuple-element.74), channel_id=1, source_target_pairs={{0,2},{1,3},{2,0},{3,1},{4,6},{5,7},{6,4},{7,5},{8,10},{9,11},{10,... | collective-permute-start | bytes 1572872 | tf_op jit(solution)/shard_map/ppermute | solution.py:32
  19.2 29.6 %collective-permute-start.5 = (bf16[512,512]{1,0:T(8,128)(2,1)}, bf16[512,512]{1,0:T(8,128)(2,1)S(1)}, u32[]{:S(2)}, u32[]{:S(2)}) collective-permute-start(bf16[512,512]{1,0:T(8,128)(2,1)} %get-tuple-element.75), channel_id=1, source_target_pairs={{0,3},{1,2},{2,1},{3,0},{4,7},{5,6},{6,5},{7,4},{8,11},{9,10},{10,... | collective-permute-start | bytes 1572872 | tf_op jit(solution)/shard_map/ppermute | solution.py:32
  19.7 25.9 %collective-permute-start.8 = (bf16[512,64]{1,0:T(8,128)(2,1)S(1)}, bf16[512,64]{1,0:T(8,128)(2,1)S(1)}, u32[]{:S(2)}, u32[]{:S(2)}) collective-permute-start(bf16[512,64]{1,0:T(8,128)(2,1)S(1)} %copy.17.refs_4_), channel_id=1, source_target_pairs={{0,3},{1,2},{2,1},{3,0},{4,7},{5,6},{6,5},{7,4},{8,11},{9,10},{10,... | collective-permute-start | bytes 196616 | tf_op jit(solution)/shard_map/ppermute | solution.py:32
  45.5 120.7 %collective-permute-start.2 = (bf16[512,1024]{1,0:T(8,128)(2,1)}, bf16[512,1024]{1,0:T(8,128)(2,1)}, u32[]{:S(2)}, u32[]{:S(2)}) collective-permute-start(bf16[512,1024]{1,0:T(8,128)(2,1)} %get-tuple-element.72), channel_id=1, source_target_pairs={{0,2},{1,3},{2,0},{3,1},{4,6},{5,7},{6,4},{7,5},{8,10},{9,11},{10,... | collective-permute-start | bytes 3145736 | tf_op jit(solution)/shard_map/ppermute | solution.py:32
  47.2 119.0 %collective-permute-start.3 = (bf16[512,1024]{1,0:T(8,128)(2,1)}, bf16[512,1024]{1,0:T(8,128)(2,1)}, u32[]{:S(2)}, u32[]{:S(2)}) collective-permute-start(bf16[512,1024]{1,0:T(8,128)(2,1)} %get-tuple-element.73), channel_id=1, source_target_pairs={{0,3},{1,2},{2,1},{3,0},{4,7},{5,6},{6,5},{7,4},{8,11},{9,10},{10,... | collective-permute-start | bytes 3145736 | tf_op jit(solution)/shard_map/ppermute | solution.py:32
  47.3 49.0 %collective-permute-start.7 = (bf16[512,64]{1,0:T(8,128)(2,1)S(1)}, bf16[512,64]{1,0:T(8,128)(2,1)S(1)}, u32[]{:S(2)}, u32[]{:S(2)}) collective-permute-start(bf16[512,64]{1,0:T(8,128)(2,1)S(1)} %copy.17.refs_4_), channel_id=1, source_target_pairs={{0,2},{1,3},{2,0},{3,1},{4,6},{5,7},{6,4},{7,5},{8,10},{9,11},{10,... | collective-permute-start | bytes 196616 | tf_op jit(solution)/shard_map/ppermute | solution.py:32
  48.8 50.4 %collective-permute-start.6 = (bf16[512,64]{1,0:T(8,128)(2,1)S(1)}, bf16[512,64]{1,0:T(8,128)(2,1)S(1)}, u32[]{:S(2)}, u32[]{:S(2)}) collective-permute-start(bf16[512,64]{1,0:T(8,128)(2,1)S(1)} %copy.17.refs_4_), channel_id=1, source_target_pairs={{0,1},{1,0},{2,3},{3,2},{4,5},{5,4},{6,7},{7,6},{8,9},{9,8},{10,11... | collective-permute-start | bytes 196616 | tf_op jit(solution)/shard_map/ppermute | solution.py:32
  96.2 98.3 %collective-permute-start.24 = (bf16[512,1024]{1,0:T(8,128)(2,1)}, bf16[512,1024]{1,0:T(8,128)(2,1)S(1)}, u32[]{:S(2)}, u32[]{:S(2)}) collective-permute-start(bf16[512,1024]{1,0:T(8,128)(2,1)} %get-tuple-element.95), channel_id=1, source_target_pairs={{0,1},{1,0},{2,3},{3,2},{4,5},{5,4},{6,7},{7,6},{8,9},{9,8},{10,11... | collective-permute-start | bytes 3145736 | tf_op jit(solution)/shard_map/ppermute | solution.py:32
  100.8 4.3 %collective-permute-start.13 = (f32[1,512]{1,0:T(1,128)}, f32[1,512]{1,0:T(1,128)S(1)}, u32[]{:S(2)}, u32[]{:S(2)}) collective-permute-start(f32[1,512]{1,0:T(1,128)} %get-tuple-element.82), channel_id=1, source_target_pairs={{0,2},{1,3},{2,0},{3,1},{4,6},{5,7},{6,4},{7,5},{8,10},{9,11},{10,... | collective-permute-start | bytes 6152 | tf_op jit(solution)/shard_map/ppermute | solution.py:32
  117.4 83.7 %collective-permute-start.25 = (bf16[512,1024]{1,0:T(8,128)(2,1)}, bf16[512,1024]{1,0:T(8,128)(2,1)}, u32[]{:S(2)}, u32[]{:S(2)}) collective-permute-start(bf16[512,1024]{1,0:T(8,128)(2,1)} %get-tuple-element.96), channel_id=1, source_target_pairs={{0,2},{1,3},{2,0},{3,1},{4,6},{5,7},{6,4},{7,5},{8,10},{9,11},{10,... | collective-permute-start | bytes 3145736 | tf_op jit(solution)/shard_map/ppermute | solution.py:32
  118.3 82.8 %collective-permute-start.26 = (bf16[512,1024]{1,0:T(8,128)(2,1)}, bf16[512,1024]{1,0:T(8,128)(2,1)}, u32[]{:S(2)}, u32[]{:S(2)}) collective-permute-start(bf16[512,1024]{1,0:T(8,128)(2,1)} %get-tuple-element.97), channel_id=1, source_target_pairs={{0,3},{1,2},{2,1},{3,0},{4,7},{5,6},{6,5},{7,4},{8,11},{9,10},{10,... | collective-permute-start | bytes 3145736 | tf_op jit(solution)/shard_map/ppermute | solution.py:32
  169.5 36.8 %collective-permute-start.21 = (bf16[512,1024]{1,0:T(8,128)(2,1)}, bf16[512,1024]{1,0:T(8,128)(2,1)S(1)}, u32[]{:S(2)}, u32[]{:S(2)}) collective-permute-start(bf16[512,1024]{1,0:T(8,128)(2,1)} %get-tuple-element.91), channel_id=1, source_target_pairs={{0,1},{1,0},{2,3},{3,2},{4,5},{5,4},{6,7},{7,6},{8,9},{9,8},{10,11... | collective-permute-start | bytes 3145736 | tf_op jit(solution)/shard_map/ppermute | solution.py:32
  173.6 61.4 %collective-permute-start.22 = (bf16[512,1024]{1,0:T(8,128)(2,1)}, bf16[512,1024]{1,0:T(8,128)(2,1)}, u32[]{:S(2)}, u32[]{:S(2)}) collective-permute-start(bf16[512,1024]{1,0:T(8,128)(2,1)} %get-tuple-element.92), channel_id=1, source_target_pairs={{0,2},{1,3},{2,0},{3,1},{4,6},{5,7},{6,4},{7,5},{8,10},{9,11},{10,... | collective-permute-start | bytes 3145736 | tf_op jit(solution)/shard_map/ppermute | solution.py:32
  194.5 40.5 %collective-permute-start.23 = (bf16[512,1024]{1,0:T(8,128)(2,1)}, bf16[512,1024]{1,0:T(8,128)(2,1)}, u32[]{:S(2)}, u32[]{:S(2)}) collective-permute-start(bf16[512,1024]{1,0:T(8,128)(2,1)} %get-tuple-element.93), channel_id=1, source_target_pairs={{0,3},{1,2},{2,1},{3,0},{4,7},{5,6},{6,5},{7,4},{8,11},{9,10},{10,... | collective-permute-start | bytes 3145736 | tf_op jit(solution)/shard_map/ppermute | solution.py:32
  204.4 34.9 %collective-permute-start.30 = (bf16[512,1024]{1,0:T(8,128)(2,1)}, bf16[512,1024]{1,0:T(8,128)(2,1)S(1)}, u32[]{:S(2)}, u32[]{:S(2)}) collective-permute-start(bf16[512,1024]{1,0:T(8,128)(2,1)} %get-tuple-element.109), channel_id=1, source_target_pairs={{0,1},{1,0},{2,3},{3,2},{4,5},{5,4},{6,7},{7,6},{8,9},{9,8},{10,11... | collective-permute-start | bytes 3145736 | tf_op jit(solution)/shard_map/ppermute | solution.py:32
  205.1 65.2 %collective-permute-start.31 = (bf16[512,1024]{1,0:T(8,128)(2,1)}, bf16[512,1024]{1,0:T(8,128)(2,1)S(1)}, u32[]{:S(2)}, u32[]{:S(2)}) collective-permute-start(bf16[512,1024]{1,0:T(8,128)(2,1)} %get-tuple-element.110), channel_id=1, source_target_pairs={{0,2},{1,3},{2,0},{3,1},{4,6},{5,7},{6,4},{7,5},{8,10},{9,11},{10,... | collective-permute-start | bytes 3145736 | tf_op jit(solution)/shard_map/ppermute | solution.py:32
  206.3 64.0 %collective-permute-start.32 = (bf16[512,1024]{1,0:T(8,128)(2,1)}, bf16[512,1024]{1,0:T(8,128)(2,1)}, u32[]{:S(2)}, u32[]{:S(2)}) collective-permute-start(bf16[512,1024]{1,0:T(8,128)(2,1)} %get-tuple-element.111), channel_id=1, source_target_pairs={{0,3},{1,2},{2,1},{3,0},{4,7},{5,6},{6,5},{7,4},{8,11},{9,10},{10,... | collective-permute-start | bytes 3145736 | tf_op jit(solution)/shard_map/ppermute | solution.py:32
  238.3 55.7 %collective-permute-start.27 = (bf16[512,1024]{1,0:T(8,128)(2,1)}, bf16[512,1024]{1,0:T(8,128)(2,1)S(1)}, u32[]{:S(2)}, u32[]{:S(2)}) collective-permute-start(bf16[512,1024]{1,0:T(8,128)(2,1)} %get-tuple-element.105), channel_id=1, source_target_pairs={{0,1},{1,0},{2,3},{3,2},{4,5},{5,4},{6,7},{7,6},{8,9},{9,8},{10,11... | collective-permute-start | bytes 3145736 | tf_op jit(solution)/shard_map/ppermute | solution.py:32
  238.3 62.5 %collective-permute-start.28 = (bf16[512,1024]{1,0:T(8,128)(2,1)}, bf16[512,1024]{1,0:T(8,128)(2,1)}, u32[]{:S(2)}, u32[]{:S(2)}) collective-permute-start(bf16[512,1024]{1,0:T(8,128)(2,1)} %get-tuple-element.106), channel_id=1, source_target_pairs={{0,2},{1,3},{2,0},{3,1},{4,6},{5,7},{6,4},{7,5},{8,10},{9,11},{10,... | collective-permute-start | bytes 3145736 | tf_op jit(solution)/shard_map/ppermute | solution.py:32
  239.3 72.1 %collective-permute-start.29 = (bf16[512,1024]{1,0:T(8,128)(2,1)}, bf16[512,1024]{1,0:T(8,128)(2,1)}, u32[]{:S(2)}, u32[]{:S(2)}) collective-permute-start(bf16[512,1024]{1,0:T(8,128)(2,1)} %get-tuple-element.107), channel_id=1, source_target_pairs={{0,3},{1,2},{2,1},{3,0},{4,7},{5,6},{6,5},{7,4},{8,11},{9,10},{10,... | collective-permute-start | bytes 3145736 | tf_op jit(solution)/shard_map/ppermute | solution.py:32
  270.3 42.8 %collective-permute-start.36 = (bf16[512,512]{1,0:T(8,128)(2,1)}, bf16[512,512]{1,0:T(8,128)(2,1)}, u32[]{:S(2)}, u32[]{:S(2)}) collective-permute-start(bf16[512,512]{1,0:T(8,128)(2,1)} %get-tuple-element.121.refs_1_), channel_id=1, source_target_pairs={{0,1},{1,0},{2,3},{3,2},{4,5},{5,4},{6,7},{7,6},{8,9},{9,8},{10,11... | collective-permute-start | bytes 1572872 | tf_op jit(solution)/shard_map/ppermute | solution.py:32
  275.3 68.4 %collective-permute-start.37 = (bf16[512,512]{1,0:T(8,128)(2,1)}, bf16[512,512]{1,0:T(8,128)(2,1)}, u32[]{:S(2)}, u32[]{:S(2)}) collective-permute-start(bf16[512,512]{1,0:T(8,128)(2,1)} %get-tuple-element.122.refs_2_), channel_id=1, source_target_pairs={{0,2},{1,3},{2,0},{3,1},{4,6},{5,7},{6,4},{7,5},{8,10},{9,11},{10,... | collective-permute-start | bytes 1572872 | tf_op jit(solution)/shard_map/ppermute | solution.py:32
  294.1 49.7 %collective-permute-start.38 = (bf16[512,512]{1,0:T(8,128)(2,1)S(1)}, bf16[512,512]{1,0:T(8,128)(2,1)}, u32[]{:S(2)}, u32[]{:S(2)}) collective-permute-start(bf16[512,512]{1,0:T(8,128)(2,1)S(1)} %copy-done.13), channel_id=1, source_target_pairs={{0,3},{1,2},{2,1},{3,0},{4,7},{5,6},{6,5},{7,4},{8,11},{9,10},{10,... | collective-permute-start | bytes 1572872 | tf_op jit(solution)/shard_map/ppermute | solution.py:32
  311.4 36.8 %collective-permute-start.33 = (bf16[512,512]{1,0:T(8,128)(2,1)S(1)}, bf16[512,512]{1,0:T(8,128)(2,1)S(1)}, u32[]{:S(2)}, u32[]{:S(2)}) collective-permute-start(bf16[512,512]{1,0:T(8,128)(2,1)S(1)} %copy-done.16), channel_id=1, source_target_pairs={{0,1},{1,0},{2,3},{3,2},{4,5},{5,4},{6,7},{7,6},{8,9},{9,8},{10,11... | collective-permute-start | bytes 1572872 | tf_op jit(solution)/shard_map/ppermute | solution.py:32
  312.0 36.1 %collective-permute-start.34 = (bf16[512,512]{1,0:T(8,128)(2,1)S(1)}, bf16[512,512]{1,0:T(8,128)(2,1)S(1)}, u32[]{:S(2)}, u32[]{:S(2)}) collective-permute-start(bf16[512,512]{1,0:T(8,128)(2,1)S(1)} %copy-done.15), channel_id=1, source_target_pairs={{0,2},{1,3},{2,0},{3,1},{4,6},{5,7},{6,4},{7,5},{8,10},{9,11},{10,... | collective-permute-start | bytes 1572872 | tf_op jit(solution)/shard_map/ppermute | solution.py:32
  313.1 43.2 %collective-permute-start.35 = (bf16[512,512]{1,0:T(8,128)(2,1)S(1)}, bf16[512,512]{1,0:T(8,128)(2,1)}, u32[]{:S(2)}, u32[]{:S(2)}) collective-permute-start(bf16[512,512]{1,0:T(8,128)(2,1)S(1)} %copy-done.14), channel_id=1, source_target_pairs={{0,3},{1,2},{2,1},{3,0},{4,7},{5,6},{6,5},{7,4},{8,11},{9,10},{10,... | collective-permute-start | bytes 1572872 | tf_op jit(solution)/shard_map/ppermute | solution.py:32
  (36 other events, 574.1 us)

commit v3 on v0

v3 whole, which is shorter than its diff:
```python
import functools

import jax
import jax.numpy as jnp
from jax import lax
from jax.experimental import pallas as pl
from jax.experimental.pallas import tpu as pltpu
from jax.sharding import PartitionSpec as P

BLOCK = 128
EPSILON = 1e-06
PARTS = (1, 2, 2, 2, 2, 2, 1, 1)
LATE = 2
AHEAD = 2
CARRIER = 3
TERMS = 3
SUMS_ROWS = 16
PARAMS = pltpu.CompilerParams(vmem_limit_bytes=56 * 2**20)


def chunk_units(total, parts):
    bounds = [0]
    whole = sum(parts)
    for i in range(len(parts)):
        bounds.append(round(total * sum(parts[: i + 1]) / whole))
    return [(a, b) for a, b in zip(bounds, bounds[1:]) if b > a]


def after(value, *others):
    return lax.optimization_barrier((value, *others))[0]


def swap(array, d, tp):
    return lax.ppermute(array, "tp", [(i, i ^ d) for i in range(tp)])


def copy_kernel(distances, me_ref, *refs):
    number = len(distances)
    outs = refs[-number:]
    rows = refs[0].shape[0]
    for i, d in enumerate(distances):
        outs[i][pl.ds(0, rows), :] = refs[i][...]
        if len(refs) > 2 * number:
            sums = refs[number][pl.ds(d, 1), :]
            height = outs[i].shape[0] - rows
            line = lax.broadcasted_iota(jnp.int32, (height, sums.shape[1]), 0)
            block = jnp.zeros((height, sums.shape[1]), jnp.float32)
            for term in range(TERMS):
                part = sums.astype(jnp.bfloat16).astype(jnp.float32)
                block = jnp.where(line == term, part, block)
                sums = sums - part
            outs[i][pl.ds(rows, height), :] = block.astype(jnp.bfloat16)


def group_spec(rows, unit, groups, first, d=0):
    return pl.BlockSpec((rows, unit), lambda j, me: (0, (me[0] ^ d) * groups + first + j))


def chunk_spec(rows, unit, first=0):
    return pl.BlockSpec((rows, unit), lambda j, me: (0, first + j))


def whole_spec(array):
    return pl.BlockSpec(array.shape, lambda j, me: (0, 0))


def cost(rows, cols, rank, passes):
    return pl.CostEstimate(
        flops=2 * rows * cols * rank, bytes_accessed=2 * passes * rows * cols, transcendentals=0
    )


def pack(me, base, tp, distances, unit, first, count, sums=None):
    rows = base.shape[0]
    groups = base.shape[1] // (tp * unit)
    number = len(distances)
    in_specs = [group_spec(rows, unit, groups, first, d) for d in distances]
    args = [base] * number
    height = rows
    if sums is not None:
        in_specs.append(chunk_spec(tp, unit))
        args.append(sums)
        height += SUMS_ROWS
    return pl.pallas_call(
        functools.partial(copy_kernel, distances),
        out_shape=[jax.ShapeDtypeStruct((height, count * unit), base.dtype)] * number,
        grid_spec=pltpu.PrefetchScalarGridSpec(
            num_scalar_prefetch=1,
            grid=(count,),
            in_specs=in_specs,
            out_specs=[chunk_spec(height, unit)] * number,
        ),
        compiler_params=PARAMS,
        cost_estimate=cost(number * rows, count * unit, 0, 2),
    )(me, *args)


def low_rank(extra_ref, start, height, right):
    left = extra_ref[pl.ds(0, right.shape[0]), pl.ds(start, height)]
    return lax.dot_general(left, right, (((0,), (0,)), ((), ())), preferred_element_type=jnp.float32)


def squares_of(piece_ref, extra_ref, right):
    rows, cols = piece_ref.shape
    height = min(rows, BLOCK)
    total = jnp.zeros((8, cols), jnp.float32)
    for r in range(0, rows, height):
        combined = piece_ref[pl.ds(r, height), :].astype(jnp.float32) + low_rank(extra_ref, r, height, right)
        total = total + jnp.sum((combined * combined).reshape(height // 8, 8, cols), axis=0)
    return total


def squares_kernel(tp, me_ref, *refs):
    pieces, extras, right_ref, out_ref = refs[:tp], refs[tp : 2 * tp], refs[-2], refs[-1]
    right = right_ref[...]
    total = sum(squares_of(piece, extra, right) for piece, extra in zip(pieces, extras))
    out_ref[...] = jnp.sum(total, axis=0, keepdims=True)


def sender_squares_kernel(tp, rank, me_ref, *refs):
    pieces, extras, out_ref = refs[:tp], refs[tp : 2 * tp], refs[-1]
    start = pl.multiple_of((1 + pl.program_id(0)) * rank, rank)
    for d in range(tp):
        right = extras[d][pl.ds(start, rank), :]
        total = squares_of(pieces[d], extras[0], right)
        out_ref[pl.ds(d, 1), :] = jnp.sum(total, axis=0, keepdims=True)


def column_squares(me, base, near, received, extras, right, unit, first, count):
    rows = base.shape[0]
    rank, cols = right.shape
    tp = len(extras)
    return pl.pallas_call(
        functools.partial(squares_kernel, tp),
        out_shape=jax.ShapeDtypeStruct((1, count * unit), jnp.float32),
        grid_spec=pltpu.PrefetchScalarGridSpec(
            num_scalar_prefetch=1,
            grid=(count,),
            in_specs=[group_spec(rows, unit, cols // unit, first), chunk_spec(rows, unit, first)]
            + [chunk_spec(rows, unit)] * (tp - 2)
            + [whole_spec(extra) for extra in extras]
            + [chunk_spec(rank, unit, first)],
            out_specs=chunk_spec(1, unit),
        ),
        compiler_params=PARAMS,
        cost_estimate=cost(tp * rows, count * unit, rank, 1),
    )(me, base, near, *received, *extras, right)


def sender_squares(me, base, extras, rank, unit, first, count):
    rows = base.shape[0]
    tp = len(extras)
    groups = base.shape[1] // (tp * unit)
    return pl.pallas_call(
        functools.partial(sender_squares_kernel, tp, rank),
        out_shape=jax.ShapeDtypeStruct((tp, count * unit), jnp.float32),
        grid_spec=pltpu.PrefetchScalarGridSpec(
            num_scalar_prefetch=1,
            grid=(count,),
            in_specs=[group_spec(rows, unit, groups, first, d) for d in range(tp)]
            + [whole_spec(extra) for extra in extras],
            out_specs=chunk_spec(tp, unit),
        ),
        compiler_params=PARAMS,
        cost_estimate=cost(tp * rows, count * unit, rank, 1),
    )(me, *[base] * tp, *extras)


def export_kernel(tp, first, me_ref, *refs):
    pieces, extras = refs[:tp], refs[tp : 2 * tp]
    right_ref, squares_ref, mag_ref = refs[2 * tp : 2 * tp + 3]
    out_ref, scales_ref = refs[-2:]
    rows, cols = pieces[0].shape
    step = pl.program_id(0)
    if len(refs) > 2 * tp + 5:
        @pl.when(step == 0)
        def _():
            scales_ref[...] = refs[2 * tp + 4][...]

    factor = mag_ref[...] / jnp.sqrt(squares_ref[...] + EPSILON)
    right = right_ref[...]
    height = min(rows, BLOCK)
    for d in range(tp):
        start = (me_ref[0] ^ d) * rows
        for r in range(0, rows, height):
            combined = pieces[d][pl.ds(r, height), :].astype(jnp.float32) + low_rank(extras[d], r, height, right)
            span = pl.ds(pl.multiple_of(start + r, height), height)
            out_ref[span, :] = (combined * factor).astype(jnp.bfloat16)

    lane = lax.broadcasted_iota(jnp.int32, (1, scales_ref.shape[1]), 1)
    per_step = cols // BLOCK
    for i in range(tp * rows // BLOCK):
        span = pl.ds(i * BLOCK, BLOCK)
        line = scales_ref[pl.ds(i, 1), :]
        for j in range(per_step):
            tile = out_ref[span, pl.ds(j * BLOCK, BLOCK)].astype(jnp.float32)
            largest = jnp.max(jnp.max(jnp.abs(tile), axis=0, keepdims=True), axis=1, keepdims=True)
            out_ref[span, pl.ds(j * BLOCK, BLOCK)] = (tile * (1.0 / (largest + EPSILON))).astype(jnp.bfloat16)
            line = jnp.where(lane == (first + step) * per_step + j, largest, line)
        scales_ref[pl.ds(i, 1), :] = line


def export_chunk(me, base, near, received, extras, right, squares, mag, unit, first, count, previous):
    rows = base.shape[0]
    rank, cols = right.shape
    tp = len(extras)
    groups = cols // unit
    result = (
        jax.ShapeDtypeStruct((tp * rows, cols), jnp.bfloat16),
        jax.ShapeDtypeStruct((tp * rows // BLOCK, cols // BLOCK), jnp.float32),
    )
    in_specs = (
        [group_spec(rows, unit, groups, first), chunk_spec(rows, unit, first)]
        + [chunk_spec(rows, unit)] * (tp - 2)
        + [whole_spec(extra) for extra in extras]
        + [chunk_spec(rank, unit, first), chunk_spec(1, unit), group_spec(1, unit, groups, first)]
    )
    args = [base, near, *received, *extras, right, squares, mag]
    aliases = {}
    if previous is not None:
        in_specs += [pl.BlockSpec(memory_space=pl.ANY), whole_spec(previous[1])]
        args += list(previous)
        aliases = {len(args) - 1: 0}
    return pl.pallas_call(
        functools.partial(export_kernel, tp, first),
        out_shape=result,
        grid_spec=pltpu.PrefetchScalarGridSpec(
            num_scalar_prefetch=1,
            grid=(count,),
            in_specs=in_specs,
            out_specs=(chunk_spec(tp * rows, unit, first), whole_spec(result[1])),
        ),
        input_output_aliases=aliases,
        compiler_params=PARAMS,
        cost_estimate=cost(tp * rows, count * unit, rank, 2),
    )(me, *args)


def body(tp, base, left, right, magnitude):
    rows, rank = left.shape
    cols = right.shape[1]
    blocks = cols // BLOCK
    unit = max(d for d in (4, 2, 1) if blocks % d == 0) * BLOCK
    chunks = chunk_units(cols // unit, PARTS)
    mag = magnitude.reshape(1, -1)
    me = lax.axis_index("tp").astype(jnp.int32).reshape(1)
    early = len(chunks) - LATE
    late_first = chunks[early][0]
    late_count = chunks[-1][1] - late_first
    far = range(2, tp)

    late_right = [right[:, u * unit : (u + 1) * unit] for u in range(late_first, late_first + late_count)]
    own = jnp.concatenate([jnp.pad(left.T, ((0, 0), (0, unit - rows)))] + late_right)
    me_first = after(me, own)
    extras = [own, swap(own, 1, tp)]
    for d in far:
        extras.append(swap(extras[d - 1], 1, tp) if d % 2 else swap(own, d, tp))

    received = {}

    def send(k, me, sums=None):
        a, b = chunks[k]
        packed = pack(me, base, tp, far, unit, a, b - a, sums)
        if k == 1:
            packed = lax.optimization_barrier((*packed, *received[0]))[: len(far)]
        received[k] = [swap(piece, d, tp) for d, piece in zip(far, packed)]
        return packed

    first = send(0, me_first)
    second = send(1, after(me, *first))
    near = pack(after(me, *second), base, tp, (1,), unit, 0, cols // unit)[0]
    near = swap(after(near, extras[-1]), 1, tp)

    result = None
    last = ()
    totals = {}
    for k in range(len(chunks)):
        a, b = chunks[k]
        following = k + AHEAD
        if following < len(chunks):
            token = last if result is None else (*last, result[1])
            turn = after(me, *received[k], *token)
            sums = None
            if following == CARRIER:
                sums = sender_squares(turn, base, extras, rank, unit, late_first, late_count)
                late = sums[:1] + swap(sums[1:2], 1, tp)
            send(following, turn, sums)
        if k < early:
            local = after(column_squares(me, base, near, received[k], extras, right, unit, a, b - a), *last)
            if k == CARRIER:
                for piece in received[k]:
                    terms = piece[rows : rows + TERMS].astype(jnp.float32)
                    late = late + jnp.sum(terms, axis=0, keepdims=True)
                totals[k], late = lax.psum((local, late), "fsdp")
                for i in range(early, len(chunks)):
                    start, end = ((u - late_first) * unit for u in chunks[i])
                    totals[i] = late[:, start:end]
            else:
                totals[k] = lax.psum(local, "fsdp")
            last = (totals[k],)
        width = unit if k < early else max(unit // 2, BLOCK)
        parts = unit // width
        result = export_chunk(
            me, base, near, received[k], extras, right, totals[k], mag, width, a * parts, (b - a) * parts, result
        )
    return result


def solution(mesh):
    in_specs = (P(("fsdp", "tp"), None), P(("fsdp", "tp"), None), P(None, "tp"), P())
    out_specs = (P("fsdp", "tp"), P("fsdp", "tp"))
    return jax.shard_map(
        functools.partial(body, mesh.shape["tp"]), mesh=mesh, in_specs=in_specs, out_specs=out_specs, check_vma=False
    )
```

time: 658 us -> 347 us (0.53)
  blocking collectives: 336 us -> 128 us
  local copies, waits for them, and re-layouts: 184 us -> 6.25 us
  Pallas kernels: 0 us -> 106 us
  other arithmetic: 98.5 us -> 2.33 us
  waiting for transfers between devices: 0.01 us -> 84.4 us
  matrix products: 27.3 us -> 0 us
  starting transfers between devices: 8.74 us -> 18.5 us
    all_gather x1 -> x0, blocking collectives: 297 us -> none  [body(): lax.all_gather(left_factor, 'tp', axis=0, tiled=True)]
    pallas_call x0 -> x24, Pallas kernels: none -> 106 us  [the longest x8 45.5 us: export_chunk(): pl.pallas_call(functools.partial(export_kernel, tp, first), out_shape=res...]
    psum x1 -> x6, blocking collectives: 38.2 us -> 128 us  [the longest x4 85.1 us: body(): totals[k] = lax.psum(local, 'fsdp')]
    ppermute x0 -> x21, waiting for transfers between devices: none -> 84.4 us  [swap(): return lax.ppermute(array, 'tp', [(i, i ^ d) for i in range(tp)])]
    div x2 -> x0, local copies, waits for them, and re-layouts: 67.7 us -> none  [to_blocks(): scaled = tile_view / (block_max[:, None, :, None] + epsilon)]
    abs x1 -> x0, local copies, waits for them, and re-layouts: 58.7 us -> none  [to_blocks(): block_max = jnp.max(jnp.abs(tile_view), axis=(1, 3))]
    convert_element_type x1 -> x0, other arithmetic: 44.2 us -> none  [to_blocks(): scaled.astype(jnp.bfloat16).reshape(row_count, col_count)]
    abs x1 -> x0, other arithmetic: 35.9 us -> none  [to_blocks(): block_max = jnp.max(jnp.abs(tile_view), axis=(1, 3))]
  transfers between devices with their start and end apart: 1 -> 21, of which waited for: 0 -> 7; matrix products, arithmetic and copies ran while one was open for 0% -> 1% of each run, Pallas kernels for 0% -> 29%
where the time goes in v3:
time: 347 us; the launch traced here: 346 us
  blocking collectives  128 us (37%)
  Pallas kernels  106 us (31%)
  waiting for transfers between devices  84.4 us (24%)
  starting transfers between devices  18.5 us (5%)
  local copies, waits for them, and re-layouts  6.25 us (2%)
    psum x4, blocking collectives, body(): totals[k] = lax.psum(local, 'fsdp')  85.1 us
    ppermute x21, waiting for transfers between devices, swap(): return lax.ppermute(array, 'tp', [(i, i ^ d) for i in range(tp)])  84.4 us
    pallas_call x8, Pallas kernels, export_chunk(): pl.pallas_call(functools.partial(export_kernel, tp, first), out_shape=res...  45.5 us
    psum x2, blocking collectives, body(): totals[k], late = lax.psum((local, late), 'fsdp')  42.4 us
    pallas_call x9, Pallas kernels, pack(): pl.pallas_call(functools.partial(copy_kernel, distances), out_shape=[jax....  31.6 us
    pallas_call x6, Pallas kernels, column_squares(): pl.pallas_call(functools.partial(squares_kernel, tp), out_shape=jax.Shape...  24.4 us
    ppermute x21, starting transfers between devices, swap(): return lax.ppermute(array, 'tp', [(i, i ^ d) for i in range(tp)])  18.5 us
  transfers between devices with their start and end apart: 21, of which 7 were waited for; matrix products, arithmetic and copies ran while one was open for 1% of the time, Pallas kernels for 29%

profile of v3, /device:TPU:0, one launch (start us, length us, event | category | flops | bytes accessed | tf_op | source)
XLA Modules:
  0.0 345.6 jit_solution(13125487347246172691)
XLA Ops:
  4.7 2.9 collective-permute-start
  8.8 26.4 %collective-permute-done.2.refs_6_ = bf16[192,512]{1,0:T(8,128)(2,1)S(1)} collective-permute-done((bf16[192,512]{1,0:T(8,128)(2,1)S(1)}, bf16[192,512]{1,0:T(8,128)(2,1)S(1)}, u32[]{:S(2)}, u32[]{:S(2)}) %collective-permute-start.2) | collective-permute-done | bytes 196640 | tf_op jit(solution)/shard_map/ppermute | solution.py:34
  38.0 10.3 %shard_map.61 = bf16[512,6656]{1,0:T(8,128)(2,1)} custom-call(s32[1]{0:T(128)} %bitcast.me_ref, bf16[512,26624]{1,0:T(8,128)(2,1)} %refs_0_.47), custom_call_target="tpu_custom_call" | custom-call | bytes 13631488 | tf_op jit(solution)/shard_map/pallas_call | solution.py:84
  55.4 4.2 %collective-permute-done.7.refs_5_ = bf16[192,512]{1,0:T(8,128)(2,1)S(1)} collective-permute-done((bf16[192,512]{1,0:T(8,128)(2,1)S(1)}, bf16[192,512]{1,0:T(8,128)(2,1)S(1)}, u32[]{:S(2)}, u32[]{:S(2)}) %collective-permute-start.7) | collective-permute-done | bytes 196640 | tf_op jit(solution)/shard_map/ppermute | solution.py:34
  61.4 2.8 copy-done
  64.2 3.1 shard_map.62
  67.3 22.4 %psum.49.refs_9_ = f32[1,512]{1,0:T(1,128)} all-reduce(f32[1,512]{1,0:T(1,128)} %shard_map.62), channel_id=1, replica_groups=mesh['fsdp'=8,'tp'=4] {'fsdp'}, use_global_device_ids=true, to_apply=%region_0.1 | all-reduce | flops 512 | bytes 4096 | tf_op jit(solution)/shard_map/psum | solution.py:299
  89.6 4.5 %shard_map.63 = (bf16[2048,6656]{1,0:T(8,128)(2,1)}, f32[16,52]{1,0:T(8,128)}) custom-call(s32[1]{0:T(128)} %bitcast.me_ref, bf16[512,26624]{1,0:T(8,128)(2,1)} %refs_0_.47, bf16[512,6656]{1,0:T(8,128)(2,1)} %copy-done, bf16[512,512]{1,0:T(8,128)(2,1)} %copy-done.10, bf16[512,512]{1,0:T(8,128)(2,1)} %copy-done.11, bf16[192,512]{1,0:T(8,128)(2,1)} %copy-done.1, ...), custom_call_target="tpu_custom_call" | custom-call | flops 134217728 | bytes 4194304 | tf_op jit(solution)/shard_map/pallas_call | solution.py:224
  96.9 4.1 %shard_map.64.refs_2_ = f32[4,1024]{1,0:T(4,128)} custom-call(s32[1]{0:T(128)} %bitcast.me_ref, bf16[512,26624]{1,0:T(8,128)(2,1)} %refs_0_.47, bf16[512,26624]{1,0:T(8,128)(2,1)} %refs_0_.47, bf16[512,26624]{1,0:T(8,128)(2,1)} %refs_0_.47, bf16[512,26624]{1,0:T(8,128)(2,1)} %refs_0_.47, bf16[192,512]{1,0:T(8,128)(2,1)} %copy-done.1, ...), custom_call_target="tpu_custom_call" | custom-call | flops 268435456 | bytes 4194304 | tf_op jit(solution)/shard_map/pallas_call | solution.py:154
  105.7 4.3 %shard_map.68 = f32[1,1024]{1,0:T(1,128)} custom-call(s32[1]{0:T(128)} %bitcast.me_ref, bf16[512,26624]{1,0:T(8,128)(2,1)} %refs_0_.47, bf16[512,6656]{1,0:T(8,128)(2,1)} %copy-done, bf16[512,1024]{1,0:T(8,128)(2,1)} %collective-permute-done.5.refs_2_, bf16[512,1024]{1,0:T(8,128)(2,1)} %collective-permute-done.6.refs_3_, bf16[192,512]{1,0:T(8,128)(2,1)} %copy-done.1, ...), custom_call_target="tpu_custom_call" | custom-call | flops 268435456 | bytes 4194304 | tf_op jit(solution)/shard_map/pallas_call | solution.py:133
  110.0 22.5 %psum.50.refs_9_ = f32[1,1024]{1,0:T(1,128)} all-reduce(f32[1,1024]{1,0:T(1,128)} %shard_map.68), channel_id=1, replica_groups=mesh['fsdp'=8,'tp'=4] {'fsdp'}, use_global_device_ids=true, to_apply=%region_1.2 | all-reduce | flops 1024 | bytes 8192 | tf_op jit(solution)/shard_map/psum | solution.py:299
  132.4 6.4 %shard_map.69 = (bf16[2048,6656]{1,0:T(8,128)(2,1)}, f32[16,52]{1,0:T(8,128)}) custom-call(s32[1]{0:T(128)} %bitcast.me_ref, bf16[512,26624]{1,0:T(8,128)(2,1)} %refs_0_.47, bf16[512,6656]{1,0:T(8,128)(2,1)} %copy-done, bf16[512,1024]{1,0:T(8,128)(2,1)} %collective-permute-done.5.refs_2_, ...), custom_call_target="tpu_custom_call", output_to_operand_aliasing={{0}: (12, {})} | custom-call | flops 268435456 | bytes 8388608 | tf_op jit(solution)/shard_map/pallas_call | solution.py:224
  138.9 3.0 collective-permute-done.11.refs_3_
  146.4 4.3 %shard_map.67 = f32[1,1024]{1,0:T(1,128)} custom-call(s32[1]{0:T(128)} %bitcast.me_ref, bf16[512,26624]{1,0:T(8,128)(2,1)} %refs_0_.47, bf16[512,6656]{1,0:T(8,128)(2,1)} %copy-done, bf16[512,1024]{1,0:T(8,128)(2,1)} %collective-permute-done.10.refs_2_, bf16[512,1024]{1,0:T(8,128)(2,1)} %collective-permute-done.11.refs_3_, bf16[192,512]{1,0:T(8,128)(2,1)} %copy-done.1, ...), custom_call_target="tpu_custom_call" | custom-call | flops 268435456 | bytes 4194304 | tf_op jit(solution)/shard_map/pallas_call | solution.py:133
  150.7 22.6 %psum.51.refs_9_ = f32[1,1024]{1,0:T(1,128)} all-reduce(f32[1,1024]{1,0:T(1,128)} %shard_map.67), channel_id=1, replica_groups=mesh['fsdp'=8,'tp'=4] {'fsdp'}, use_global_device_ids=true, to_apply=%region_2.3 | all-reduce | flops 1024 | bytes 8192 | tf_op jit(solution)/shard_map/psum | solution.py:299
  173.3 6.4 %shard_map.70 = (bf16[2048,6656]{1,0:T(8,128)(2,1)}, f32[16,52]{1,0:T(8,128)}) custom-call(s32[1]{0:T(128)} %bitcast.me_ref, bf16[512,26624]{1,0:T(8,128)(2,1)} %refs_0_.47, bf16[512,6656]{1,0:T(8,128)(2,1)} %copy-done, bf16[512,1024]{1,0:T(8,128)(2,1)} %collective-permute-done.10.refs_2_, ...), custom_call_target="tpu_custom_call", output_to_operand_aliasing={{0}: (12, {})} | custom-call | flops 268435456 | bytes 8388608 | tf_op jit(solution)/shard_map/pallas_call | solution.py:224
  179.7 8.5 %collective-permute-done.9.refs_3_ = bf16[528,1024]{1,0:T(8,128)(2,1)S(1)} collective-permute-done((bf16[528,1024]{1,0:T(8,128)(2,1)}, bf16[528,1024]{1,0:T(8,128)(2,1)S(1)}, u32[]{:S(2)}, u32[]{:S(2)}) %collective-permute-start.9) | collective-permute-done | bytes 1081376 | tf_op jit(solution)/shard_map/ppermute | solution.py:34
  188.2 3.0 shard_map.71
  193.5 17.8 %collective-permute-done.14.refs_2_ = bf16[512,1024]{1,0:T(8,128)(2,1)S(1)} collective-permute-done((bf16[512,1024]{1,0:T(8,128)(2,1)}, bf16[512,1024]{1,0:T(8,128)(2,1)S(1)}, u32[]{:S(2)}, u32[]{:S(2)}) %collective-permute-start.14) | collective-permute-done | bytes 1048608 | tf_op jit(solution)/shard_map/ppermute | solution.py:34
  211.3 21.8 %collective-permute-done.15.refs_3_ = bf16[512,1024]{1,0:T(8,128)(2,1)} collective-permute-done((bf16[512,1024]{1,0:T(8,128)(2,1)}, bf16[512,1024]{1,0:T(8,128)(2,1)}, u32[]{:S(2)}, u32[]{:S(2)}) %collective-permute-start.15) | collective-permute-done | bytes 1048608 | tf_op jit(solution)/shard_map/ppermute | solution.py:34
  233.1 4.2 %shard_map.73 = f32[1,1024]{1,0:T(1,128)} custom-call(s32[1]{0:T(128)} %bitcast.me_ref, bf16[512,26624]{1,0:T(8,128)(2,1)} %refs_0_.47, bf16[512,6656]{1,0:T(8,128)(2,1)} %copy-done, bf16[512,1024]{1,0:T(8,128)(2,1)} %copy-done.9, bf16[512,1024]{1,0:T(8,128)(2,1)} %collective-permute-done.15.refs_3_, bf16[192,512]{1,0:T(8,128)(2,1)} %copy-done.1, ...), custom_call_target="tpu_custom_call" | custom-call | flops 268435456 | bytes 4194304 | tf_op jit(solution)/shard_map/pallas_call | solution.py:133
  237.4 4.3 %shard_map.74 = f32[1,1024]{1,0:T(1,128)} custom-call(s32[1]{0:T(128)} %bitcast.me_ref, bf16[512,26624]{1,0:T(8,128)(2,1)} %refs_0_.47, bf16[512,6656]{1,0:T(8,128)(2,1)} %copy-done, bf16[528,1024]{1,0:T(8,128)(2,1)} %copy-done.6, bf16[528,1024]{1,0:T(8,128)(2,1)} %copy-done.5, bf16[192,512]{1,0:T(8,128)(2,1)} %copy-done.1, bf16[192,512]{1,0:T(8,128)(2,1)} %copy-done.4, ...), custom_call_target="tpu_custom_call" | custom-call | flops 268435456 | bytes 4194304 | tf_op jit(solution)/shard_map/pallas_call | solution.py:133
  241.7 22.4 %psum.52.refs_9_ = f32[1,1024]{1,0:T(1,128)} all-reduce(f32[1,1024]{1,0:T(1,128)} %shard_map.74), channel_id=1, replica_groups=mesh['fsdp'=8,'tp'=4] {'fsdp'}, use_global_device_ids=true, to_apply=%region_3.4 | all-reduce | flops 1024 | bytes 8192 | tf_op jit(solution)/shard_map/psum | solution.py:294
  264.1 6.4 %shard_map.75 = (bf16[2048,6656]{1,0:T(8,128)(2,1)}, f32[16,52]{1,0:T(8,128)}) custom-call(s32[1]{0:T(128)} %bitcast.me_ref, bf16[512,26624]{1,0:T(8,128)(2,1)} %refs_0_.47, bf16[512,6656]{1,0:T(8,128)(2,1)} %copy-done, bf16[528,1024]{1,0:T(8,128)(2,1)} %copy-done.6, bf16[528,1024]{1,0:T(8,128)(2,1)} %copy-done.5, ...), custom_call_target="tpu_custom_call", output_to_operand_aliasing={{0}: (12, {})} | custom-call | flops 268435456 | bytes 8388608 | tf_op jit(solution)/shard_map/pallas_call | solution.py:224
  273.5 17.7 %psum.53.refs_9_ = f32[1,1024]{1,0:T(1,128)} all-reduce(f32[1,1024]{1,0:T(1,128)S(1)} %copy-done.17), channel_id=1, replica_groups=mesh['fsdp'=8,'tp'=4] {'fsdp'}, use_global_device_ids=true, to_apply=%region_4.5 | all-reduce | flops 1024 | bytes 8192 | tf_op jit(solution)/shard_map/psum | solution.py:299
  291.3 6.4 %shard_map.76 = (bf16[2048,6656]{1,0:T(8,128)(2,1)}, f32[16,52]{1,0:T(8,128)}) custom-call(s32[1]{0:T(128)} %bitcast.me_ref, bf16[512,26624]{1,0:T(8,128)(2,1)} %refs_0_.47, bf16[512,6656]{1,0:T(8,128)(2,1)} %copy-done, bf16[512,1024]{1,0:T(8,128)(2,1)} %copy-done.9, ...), custom_call_target="tpu_custom_call", output_to_operand_aliasing={{0}: (12, {})} | custom-call | flops 268435456 | bytes 8388608 | tf_op jit(solution)/shard_map/pallas_call | solution.py:224
  298.5 3.0 shard_map.77
  303.5 4.3 %shard_map.79 = f32[1,1024]{1,0:T(1,128)} custom-call(s32[1]{0:T(128)} %bitcast.me_ref, bf16[512,26624]{1,0:T(8,128)(2,1)} %refs_0_.47, bf16[512,6656]{1,0:T(8,128)(2,1)} %copy-done, bf16[512,1024]{1,0:T(8,128)(2,1)} %copy-done.7, bf16[512,1024]{1,0:T(8,128)(2,1)} %copy-done.8, bf16[192,512]{1,0:T(8,128)(2,1)} %copy-done.1, bf16[192,512]{1,0:T(8,128)(2,1)} %copy-done.4, ...), custom_call_target="tpu_custom_call" | custom-call | flops 268435456 | bytes 4194304 | tf_op jit(solution)/shard_map/pallas_call | solution.py:133
  307.8 20.0 %all-reduce = (f32[1,1024]{1,0:T(1,128)S(1)}, f32[1,1024]{1,0:T(1,128)}) all-reduce(f32[1,1024]{1,0:T(1,128)S(1)} %fusion.1, f32[1,1024]{1,0:T(1,128)} %shard_map.79), channel_id=1, replica_groups=mesh['fsdp'=8,'tp'=4] {'fsdp'}, use_global_device_ids=true, to_apply=%region_7.8 | all-reduce | flops 2048 | bytes 16384 | tf_op jit(solution)/shard_map/psum | solution.py:294
  327.8 6.4 %shard_map.80 = (bf16[2048,6656]{1,0:T(8,128)(2,1)}, f32[16,52]{1,0:T(8,128)}) custom-call(s32[1]{0:T(128)} %bitcast.me_ref, bf16[512,26624]{1,0:T(8,128)(2,1)} %refs_0_.47, bf16[512,6656]{1,0:T(8,128)(2,1)} %copy-done, bf16[512,1024]{1,0:T(8,128)(2,1)} %copy-done.7, bf16[512,1024]{1,0:T(8,128)(2,1)} %copy-done.8, ...), custom_call_target="tpu_custom_call", output_to_operand_aliasing={{0}: (12, {})} | custom-call | flops 268435456 | bytes 8388608 | tf_op jit(solution)/shard_map/pallas_call | solution.py:224
  335.8 4.4 %shard_map.81 = (bf16[2048,6656]{1,0:T(8,128)(2,1)}, f32[16,52]{1,0:T(8,128)}) custom-call(s32[1]{0:T(128)} %bitcast.me_ref, bf16[512,26624]{1,0:T(8,128)(2,1)} %refs_0_.47, bf16[512,6656]{1,0:T(8,128)(2,1)} %copy-done, bf16[512,512]{1,0:T(8,128)(2,1)} %copy-done.12, bf16[512,512]{1,0:T(8,128)(2,1)} %copy-done.13, ...), custom_call_target="tpu_custom_call", output_to_operand_aliasing={{0}: (12, {})} | custom-call | flops 134217728 | bytes 4194304 | tf_op jit(solution)/shard_map/pallas_call | solution.py:224
  341.2 4.4 %shard_map.82 = (bf16[2048,6656]{1,0:T(8,128)(2,1)}, f32[16,52]{1,0:T(8,128)}) custom-call(s32[1]{0:T(128)} %bitcast.me_ref, bf16[512,26624]{1,0:T(8,128)(2,1)} %refs_0_.47, bf16[512,6656]{1,0:T(8,128)(2,1)} %copy-done, bf16[512,512]{1,0:T(8,128)(2,1)} %copy-done.14, bf16[512,512]{1,0:T(8,128)(2,1)} %copy-done.15, ...), custom_call_target="tpu_custom_call", output_to_operand_aliasing={{0}: (12, {})} | custom-call | flops 134217728 | bytes 4194304 | tf_op jit(solution)/shard_map/pallas_call | solution.py:224
  (83 shorter events, 39.4 us)
Async XLA Ops:
  2.4 48.2 %copy-start.1 = (bf16[192,512]{1,0:T(8,128)(2,1)}, bf16[192,512]{1,0:T(8,128)(2,1)S(1)}, u32[]{:S(2)}) copy-start(bf16[192,512]{1,0:T(8,128)(2,1)S(1)} %pad_maximum_fusion.refs_4_) | copy-start | bytes 589828
  4.7 33.3 %collective-permute-start = (bf16[512,512]{1,0:T(8,128)(2,1)}, bf16[512,512]{1,0:T(8,128)(2,1)S(1)}, u32[]{:S(2)}, u32[]{:S(2)}) collective-permute-start(bf16[512,512]{1,0:T(8,128)(2,1)} %get-tuple-element.50), channel_id=1, source_target_pairs={{0,2},{1,3},{2,0},{3,1},{4,6},{5,7},{6,4},{7,5},{8,10},{9,11},{10,... | collective-permute-start | bytes 1572872 | tf_op jit(solution)/shard_map/ppermute | solution.py:34
  7.6 30.4 %collective-permute-start.1 = (bf16[512,512]{1,0:T(8,128)(2,1)}, bf16[512,512]{1,0:T(8,128)(2,1)S(1)}, u32[]{:S(2)}, u32[]{:S(2)}) collective-permute-start(bf16[512,512]{1,0:T(8,128)(2,1)} %get-tuple-element.51), channel_id=1, source_target_pairs={{0,3},{1,2},{2,1},{3,0},{4,7},{5,6},{6,5},{7,4},{8,11},{9,10},{10,... | collective-permute-start | bytes 1572872 | tf_op jit(solution)/shard_map/ppermute | solution.py:34
  7.6 27.6 %collective-permute-start.2 = (bf16[192,512]{1,0:T(8,128)(2,1)S(1)}, bf16[192,512]{1,0:T(8,128)(2,1)S(1)}, u32[]{:S(2)}, u32[]{:S(2)}) collective-permute-start(bf16[192,512]{1,0:T(8,128)(2,1)S(1)} %pad_maximum_fusion.refs_4_), channel_id=1, source_target_pairs={{0,2},{1,3},{2,0},{3,1},{4,6},{5,7},{6,4},{7,5},{8,10},{9,11},{10,... | collective-permute-start | bytes 589832 | tf_op jit(solution)/shard_map/ppermute | solution.py:34
  35.2 13.1 %collective-permute-start.3 = (bf16[192,512]{1,0:T(8,128)(2,1)S(1)}, bf16[192,512]{1,0:T(8,128)(2,1)S(1)}, u32[]{:S(2)}, u32[]{:S(2)}) collective-permute-start(bf16[192,512]{1,0:T(8,128)(2,1)S(1)} %collective-permute-done.2.refs_6_), channel_id=1, source_target_pairs={{0,1},{1,0},{2,3},{3,2},{4,5},{5,4},{6,7},{7,6},{8,9},{9,8},{10,11... | collective-permute-start | bytes 589832 | tf_op jit(solution)/shard_map/ppermute | solution.py:34
  38.0 15.7 %copy-start.10 = (bf16[512,512]{1,0:T(8,128)(2,1)}, bf16[512,512]{1,0:T(8,128)(2,1)S(1)}, u32[]{:S(2)}) copy-start(bf16[512,512]{1,0:T(8,128)(2,1)S(1)} %collective-permute-done.refs_2_) | copy-start | bytes 1572868
  38.0 10.3 %copy-start.11 = (bf16[512,512]{1,0:T(8,128)(2,1)}, bf16[512,512]{1,0:T(8,128)(2,1)S(1)}, u32[]{:S(2)}) copy-start(bf16[512,512]{1,0:T(8,128)(2,1)S(1)} %collective-permute-done.1.refs_3_) | copy-start | bytes 1572868
  48.3 5.3 %copy-start.3 = (bf16[192,512]{1,0:T(8,128)(2,1)}, bf16[192,512]{1,0:T(8,128)(2,1)S(1)}, u32[]{:S(2)}) copy-start(bf16[192,512]{1,0:T(8,128)(2,1)S(1)} %collective-permute-done.3.refs_7_) | copy-start | bytes 589828
  48.3 13.0 %collective-permute-start.4 = (bf16[512,6656]{1,0:T(8,128)(2,1)}, bf16[512,6656]{1,0:T(8,128)(2,1)S(1)}, u32[]{:S(2)}, u32[]{:S(2)}) collective-permute-start(bf16[512,6656]{1,0:T(8,128)(2,1)} %shard_map.61), channel_id=1, source_target_pairs={{0,1},{1,0},{2,3},{3,2},{4,5},{5,4},{6,7},{7,6},{8,9},{9,8},{10,11... | collective-permute-start | bytes 20447240 | tf_op jit(solution)/shard_map/ppermute | solution.py:34
  48.8 45.3 %collective-permute-start.5 = (bf16[512,1024]{1,0:T(8,128)(2,1)}, bf16[512,1024]{1,0:T(8,128)(2,1)}, u32[]{:S(2)}, u32[]{:S(2)}) collective-permute-start(bf16[512,1024]{1,0:T(8,128)(2,1)} %get-tuple-element.55), channel_id=1, source_target_pairs={{0,2},{1,3},{2,0},{3,1},{4,6},{5,7},{6,4},{7,5},{8,10},{9,11},{10,... | collective-permute-start | bytes 3145736 | tf_op jit(solution)/shard_map/ppermute | solution.py:34
  50.6 46.3 %collective-permute-start.6 = (bf16[512,1024]{1,0:T(8,128)(2,1)}, bf16[512,1024]{1,0:T(8,128)(2,1)}, u32[]{:S(2)}, u32[]{:S(2)}) collective-permute-start(bf16[512,1024]{1,0:T(8,128)(2,1)} %get-tuple-element.56), channel_id=1, source_target_pairs={{0,3},{1,2},{2,1},{3,0},{4,7},{5,6},{6,5},{7,4},{8,11},{9,10},{10,... | collective-permute-start | bytes 3145736 | tf_op jit(solution)/shard_map/ppermute | solution.py:34
  50.6 9.1 %collective-permute-start.7 = (bf16[192,512]{1,0:T(8,128)(2,1)S(1)}, bf16[192,512]{1,0:T(8,128)(2,1)S(1)}, u32[]{:S(2)}, u32[]{:S(2)}) collective-permute-start(bf16[192,512]{1,0:T(8,128)(2,1)S(1)} %pad_maximum_fusion.refs_4_), channel_id=1, source_target_pairs={{0,1},{1,0},{2,3},{3,2},{4,5},{5,4},{6,7},{7,6},{8,9},{9,8},{10,11... | collective-permute-start | bytes 589832 | tf_op jit(solution)/shard_map/ppermute | solution.py:34
  53.6 85.2 %collective-permute-start.10 = (bf16[512,1024]{1,0:T(8,128)(2,1)}, bf16[512,1024]{1,0:T(8,128)(2,1)}, u32[]{:S(2)}, u32[]{:S(2)}) collective-permute-start(bf16[512,1024]{1,0:T(8,128)(2,1)} %get-tuple-element.64), channel_id=1, source_target_pairs={{0,2},{1,3},{2,0},{3,1},{4,6},{5,7},{6,4},{7,5},{8,10},{9,11},{10,... | collective-permute-start | bytes 3145736 | tf_op jit(solution)/shard_map/ppermute | solution.py:34
  59.7 82.2 %collective-permute-start.11 = (bf16[512,1024]{1,0:T(8,128)(2,1)}, bf16[512,1024]{1,0:T(8,128)(2,1)}, u32[]{:S(2)}, u32[]{:S(2)}) collective-permute-start(bf16[512,1024]{1,0:T(8,128)(2,1)} %get-tuple-element.65), channel_id=1, source_target_pairs={{0,3},{1,2},{2,1},{3,0},{4,7},{5,6},{6,5},{7,4},{8,11},{9,10},{10,... | collective-permute-start | bytes 3145736 | tf_op jit(solution)/shard_map/ppermute | solution.py:34
  103.7 76.0 %collective-permute-start.8 = (bf16[528,1024]{1,0:T(8,128)(2,1)}, bf16[528,1024]{1,0:T(8,128)(2,1)S(1)}, u32[]{:S(2)}, u32[]{:S(2)}) collective-permute-start(bf16[528,1024]{1,0:T(8,128)(2,1)} %get-tuple-element.61), channel_id=1, source_target_pairs={{0,2},{1,3},{2,0},{3,1},{4,6},{5,7},{6,4},{7,5},{8,10},{9,11},{10,... | collective-permute-start | bytes 3244040 | tf_op jit(solution)/shard_map/ppermute | solution.py:34
  104.5 83.7 %collective-permute-start.9 = (bf16[528,1024]{1,0:T(8,128)(2,1)}, bf16[528,1024]{1,0:T(8,128)(2,1)S(1)}, u32[]{:S(2)}, u32[]{:S(2)}) collective-permute-start(bf16[528,1024]{1,0:T(8,128)(2,1)} %get-tuple-element.62), channel_id=1, source_target_pairs={{0,3},{1,2},{2,1},{3,0},{4,7},{5,6},{6,5},{7,4},{8,11},{9,10},{10,... | collective-permute-start | bytes 3244040 | tf_op jit(solution)/shard_map/ppermute | solution.py:34
  144.5 66.8 %collective-permute-start.14 = (bf16[512,1024]{1,0:T(8,128)(2,1)}, bf16[512,1024]{1,0:T(8,128)(2,1)S(1)}, u32[]{:S(2)}, u32[]{:S(2)}) collective-permute-start(bf16[512,1024]{1,0:T(8,128)(2,1)} %get-tuple-element.76), channel_id=1, source_target_pairs={{0,2},{1,3},{2,0},{3,1},{4,6},{5,7},{6,4},{7,5},{8,10},{9,11},{10,... | collective-permute-start | bytes 3145736 | tf_op jit(solution)/shard_map/ppermute | solution.py:34
  145.2 87.9 %collective-permute-start.15 = (bf16[512,1024]{1,0:T(8,128)(2,1)}, bf16[512,1024]{1,0:T(8,128)(2,1)}, u32[]{:S(2)}, u32[]{:S(2)}) collective-permute-start(bf16[512,1024]{1,0:T(8,128)(2,1)} %get-tuple-element.77), channel_id=1, source_target_pairs={{0,3},{1,2},{2,1},{3,0},{4,7},{5,6},{6,5},{7,4},{8,11},{9,10},{10,... | collective-permute-start | bytes 3145736 | tf_op jit(solution)/shard_map/ppermute | solution.py:34
  179.7 11.5 %copy-start.6 = (bf16[528,1024]{1,0:T(8,128)(2,1)}, bf16[528,1024]{1,0:T(8,128)(2,1)S(1)}, u32[]{:S(2)}) copy-start(bf16[528,1024]{1,0:T(8,128)(2,1)S(1)} %collective-permute-done.8.refs_2_) | copy-start | bytes 3244036
  188.2 3.0 copy-start.5
  188.2 5.0 %copy-start.16 = (f32[4,1024]{1,0:T(4,128)S(1)}, f32[4,1024]{1,0:T(4,128)}, u32[]{:S(2)}) copy-start(f32[4,1024]{1,0:T(4,128)} %shard_map.64.refs_2_) | copy-start | bytes 49156
  191.2 107.2 %collective-permute-start.12 = (bf16[512,1024]{1,0:T(8,128)(2,1)}, bf16[512,1024]{1,0:T(8,128)(2,1)S(1)}, u32[]{:S(2)}, u32[]{:S(2)}) collective-permute-start(bf16[512,1024]{1,0:T(8,128)(2,1)} %get-tuple-element.73), channel_id=1, source_target_pairs={{0,2},{1,3},{2,0},{3,1},{4,6},{5,7},{6,4},{7,5},{8,10},{9,11},{10,... | collective-permute-start | bytes 3145736 | tf_op jit(solution)/shard_map/ppermute | solution.py:34
  191.9 106.5 %collective-permute-start.13 = (bf16[512,1024]{1,0:T(8,128)(2,1)}, bf16[512,1024]{1,0:T(8,128)(2,1)S(1)}, u32[]{:S(2)}, u32[]{:S(2)}) collective-permute-start(bf16[512,1024]{1,0:T(8,128)(2,1)} %get-tuple-element.74), channel_id=1, source_target_pairs={{0,3},{1,2},{2,1},{3,0},{4,7},{5,6},{6,5},{7,4},{8,11},{9,10},{10,... | collective-permute-start | bytes 3145736 | tf_op jit(solution)/shard_map/ppermute | solution.py:34
  193.2 110.3 %collective-permute-start.18 = (f32[1,1024]{1,0:T(1,128)S(1)}, f32[1,1024]{1,0:T(1,128)S(1)}, u32[]{:S(2)}, u32[]{:S(2)}) collective-permute-start(f32[1,1024]{1,0:T(1,128)S(1)} %slice.33), channel_id=1, source_target_pairs={{0,1},{1,0},{2,3},{3,2},{4,5},{5,4},{6,7},{7,6},{8,9},{9,8},{10,11... | collective-permute-start | bytes 12296 | tf_op jit(solution)/shard_map/ppermute | solution.py:34
  211.3 21.8 %copy-start.9 = (bf16[512,1024]{1,0:T(8,128)(2,1)}, bf16[512,1024]{1,0:T(8,128)(2,1)S(1)}, u32[]{:S(2)}) copy-start(bf16[512,1024]{1,0:T(8,128)(2,1)S(1)} %collective-permute-done.14.refs_2_) | copy-start | bytes 3145732
  270.5 3.0 copy-start.17
  272.8 62.0 %collective-permute-start.19 = (bf16[512,512]{1,0:T(8,128)(2,1)}, bf16[512,512]{1,0:T(8,128)(2,1)S(1)}, u32[]{:S(2)}, u32[]{:S(2)}) collective-permute-start(bf16[512,512]{1,0:T(8,128)(2,1)} %get-tuple-element.88), channel_id=1, source_target_pairs={{0,2},{1,3},{2,0},{3,1},{4,6},{5,7},{6,4},{7,5},{8,10},{9,11},{10,... | collective-permute-start | bytes 1572872 | tf_op jit(solution)/shard_map/ppermute | solution.py:34
  273.5 61.2 %collective-permute-start.20 = (bf16[512,512]{1,0:T(8,128)(2,1)}, bf16[512,512]{1,0:T(8,128)(2,1)S(1)}, u32[]{:S(2)}, u32[]{:S(2)}) collective-permute-start(bf16[512,512]{1,0:T(8,128)(2,1)} %get-tuple-element.89), channel_id=1, source_target_pairs={{0,3},{1,2},{2,1},{3,0},{4,7},{5,6},{6,5},{7,4},{8,11},{9,10},{10,... | collective-permute-start | bytes 1572872 | tf_op jit(solution)/shard_map/ppermute | solution.py:34
  298.4 3.0 copy-start.7
  298.5 3.0 copy-start.8
  301.4 38.7 %collective-permute-start.16 = (bf16[512,512]{1,0:T(8,128)(2,1)}, bf16[512,512]{1,0:T(8,128)(2,1)S(1)}, u32[]{:S(2)}, u32[]{:S(2)}) collective-permute-start(bf16[512,512]{1,0:T(8,128)(2,1)} %get-tuple-element.85), channel_id=1, source_target_pairs={{0,2},{1,3},{2,0},{3,1},{4,6},{5,7},{6,4},{7,5},{8,10},{9,11},{10,... | collective-permute-start | bytes 1572872 | tf_op jit(solution)/shard_map/ppermute | solution.py:34
  302.7 37.5 %collective-permute-start.17 = (bf16[512,512]{1,0:T(8,128)(2,1)}, bf16[512,512]{1,0:T(8,128)(2,1)S(1)}, u32[]{:S(2)}, u32[]{:S(2)}) collective-permute-start(bf16[512,512]{1,0:T(8,128)(2,1)} %get-tuple-element.86), channel_id=1, source_target_pairs={{0,3},{1,2},{2,1},{3,0},{4,7},{5,6},{6,5},{7,4},{8,11},{9,10},{10,... | collective-permute-start | bytes 1572872 | tf_op jit(solution)/shard_map/ppermute | solution.py:34
  (7 other events, 10.8 us)

commit v4 on v3

--- a/solution.py
+++ b/solution.py
@@ -9,9 +9,10 @@
 
 BLOCK = 128
 EPSILON = 1e-06
-PARTS = (1, 2, 2, 2, 2, 2, 1, 1)
+PARTS = (3, 3, 3, 2, 1, 1)
 LATE = 2
 AHEAD = 2
+SCALE = 3
 CARRIER = 3
 TERMS = 3
 SUMS_ROWS = 16
@@ -34,22 +35,46 @@
     return lax.ppermute(array, "tp", [(i, i ^ d) for i in range(tp)])
 
 
-def copy_kernel(distances, me_ref, *refs):
-    number = len(distances)
-    outs = refs[-number:]
-    rows = refs[0].shape[0]
-    for i, d in enumerate(distances):
-        outs[i][pl.ds(0, rows), :] = refs[i][...]
-        if len(refs) > 2 * number:
-            sums = refs[number][pl.ds(d, 1), :]
-            height = outs[i].shape[0] - rows
-            line = lax.broadcasted_iota(jnp.int32, (height, sums.shape[1]), 0)
-            block = jnp.zeros((height, sums.shape[1]), jnp.float32)
-            for term in range(TERMS):
-                part = sums.astype(jnp.bfloat16).astype(jnp.float32)
-                block = jnp.where(line == term, part, block)
-                sums = sums - part
-            outs[i][pl.ds(rows, height), :] = block.astype(jnp.bfloat16)
+def copy_kernel(number, me_ref, *refs):
+    for source, target in zip(refs[:number], refs[number:]):
+        target[...] = source[...]
+
+
+def first_kernel(far, me_ref, *refs):
+    pieces, (left, right), outs = refs[: len(far)], refs[len(far) : len(far) + 2], refs[len(far) + 2 :]
+    own = outs[-1]
+    rows = pieces[0].shape[0]
+    step = pl.program_id(0)
+
+    @pl.when(step == 0)
+    def _():
+        if left.shape[1] < own.shape[1]:
+            own[...] = jnp.zeros_like(own)
+        own[:, pl.ds(0, left.shape[1])] = left[...]
+
+    @pl.when(step > 0)
+    def _():
+        own[...] = right[...]
+
+    for d, piece, out in zip(far, pieces, outs):
+        out[pl.ds(0, rows), :] = piece[...]
+        if d % 2 == 0:
+            out[pl.ds(rows, own.shape[0]), :] = own[...]
+
+
+def carrier_kernel(far, me_ref, *refs):
+    pieces, sums_ref, outs = refs[: len(far)], refs[len(far)], refs[len(far) + 1 :]
+    rows, cols = pieces[0].shape
+    line = lax.broadcasted_iota(jnp.int32, (SUMS_ROWS, cols), 0)
+    for d, piece, out in zip(far, pieces, outs):
+        out[pl.ds(0, rows), :] = piece[...]
+        rest = sums_ref[pl.ds(d, 1), :]
+        block = jnp.zeros((SUMS_ROWS, cols), jnp.float32)
+        for term in range(TERMS):
+            part = rest.astype(jnp.bfloat16).astype(jnp.float32)
+            block = jnp.where(line == term, part, block)
+            rest = rest - part
+        out[pl.ds(rows, SUMS_ROWS), :] = block.astype(jnp.bfloat16)
 
 
 def group_spec(rows, unit, groups, first, d=0):
@@ -60,39 +85,98 @@
     return pl.BlockSpec((rows, unit), lambda j, me: (0, first + j))
 
 
+def left_spec(rank, unit):
+    return pl.BlockSpec((rank, unit), lambda j, me: (0, 0))
+
+
 def whole_spec(array):
     return pl.BlockSpec(array.shape, lambda j, me: (0, 0))
 
 
 def cost(rows, cols, rank, passes):
     return pl.CostEstimate(
-        flops=2 * rows * cols * rank, bytes_accessed=2 * passes * rows * cols, transcendentals=0
+        flops=2 * rows * cols * rank // SCALE, bytes_accessed=2 * passes * rows * cols // SCALE, transcendentals=0
     )
 
 
-def pack(me, base, tp, distances, unit, first, count, sums=None):
+def pack(me, base, tp, distances, unit, first, count):
     rows = base.shape[0]
     groups = base.shape[1] // (tp * unit)
     number = len(distances)
-    in_specs = [group_spec(rows, unit, groups, first, d) for d in distances]
-    args = [base] * number
-    height = rows
-    if sums is not None:
-        in_specs.append(chunk_spec(tp, unit))
-        args.append(sums)
-        height += SUMS_ROWS
-    return pl.pallas_call(
-        functools.partial(copy_kernel, distances),
-        out_shape=[jax.ShapeDtypeStruct((height, count * unit), base.dtype)] * number,
-        grid_spec=pltpu.PrefetchScalarGridSpec(
-            num_scalar_prefetch=1,
-            grid=(count,),
-            in_specs=in_specs,
-            out_specs=[chunk_spec(height, unit)] * number,
+    return pl.pallas_call(
+        functools.partial(copy_kernel, number),
+        out_shape=[jax.ShapeDtypeStruct((rows, count * unit), base.dtype)] * number,
+        grid_spec=pltpu.PrefetchScalarGridSpec(
+            num_scalar_prefetch=1,
+            grid=(count,),
+            in_specs=[group_spec(rows, unit, groups, first, d) for d in distances],
+            out_specs=[chunk_spec(rows, unit)] * number,
         ),
         compiler_params=PARAMS,
         cost_estimate=cost(number * rows, count * unit, 0, 2),
-    )(me, *args)
+    )(me, *[base] * number)
+
+
+def pack_near(me, base, tp):
+    rows = base.shape[0]
+    cols = base.shape[1] // tp
+    height = max(rows // 4, 16)
+    steps = rows // height
+    return pl.pallas_call(
+        functools.partial(copy_kernel, 1),
+        out_shape=jax.ShapeDtypeStruct((2 * rows, cols), base.dtype),
+        grid_spec=pltpu.PrefetchScalarGridSpec(
+            num_scalar_prefetch=1,
+            grid=(2, steps),
+            in_specs=[pl.BlockSpec((height, cols), lambda s, i, me: (i, (me[0] // 2) * 2 + s))],
+            out_specs=pl.BlockSpec((height, cols), lambda s, i, me: (s * steps + i, 0)),
+        ),
+        compiler_params=PARAMS,
+        cost_estimate=cost(rows, cols, 0, 2),
+    )(me, base)
+
+
+def near_spec(rows, unit, first):
+    return pl.BlockSpec((rows, unit), lambda j, me: ((me[0] % 2) ^ 1, first + j))
+
+
+def pack_first(me, base, tp, far, left, right, unit, late):
+    rows, rank = left.shape
+    groups = base.shape[1] // (tp * unit)
+    count = 1 + len(late)
+    shapes = [(rows + (rank if d % 2 == 0 else 0), unit) for d in far] + [(rank, unit)]
+    return pl.pallas_call(
+        functools.partial(first_kernel, far),
+        out_shape=[jax.ShapeDtypeStruct((height, count * unit), base.dtype) for height, _ in shapes],
+        grid_spec=pltpu.PrefetchScalarGridSpec(
+            num_scalar_prefetch=1,
+            grid=(count,),
+            in_specs=[group_spec(rows, unit, groups, 0, d) for d in far]
+            + [left_spec(rank, rows), chunk_spec(rank, unit, late[0] - 1)],
+            out_specs=[chunk_spec(*shape) for shape in shapes],
+        ),
+        compiler_params=PARAMS,
+        cost_estimate=cost(len(far) * rows, count * unit, 0, 2),
+    )(me, *[base] * len(far), left.T, right)
+
+
+def pack_carrier(me, base, tp, far, sums, unit, first, count):
+    rows = base.shape[0]
+    groups = base.shape[1] // (tp * unit)
+    width = sums.shape[1] // unit
+    return pl.pallas_call(
+        functools.partial(carrier_kernel, far),
+        out_shape=[jax.ShapeDtypeStruct((rows + SUMS_ROWS, count * unit), base.dtype)] * len(far),
+        grid_spec=pltpu.PrefetchScalarGridSpec(
+            num_scalar_prefetch=1,
+            grid=(count,),
+            in_specs=[group_spec(rows, unit, groups, first, d) for d in far]
+            + [pl.BlockSpec((tp, unit), lambda j, me: (0, jnp.minimum(j, width - 1)))],
+            out_specs=[chunk_spec(rows + SUMS_ROWS, unit)] * len(far),
+        ),
+        compiler_params=PARAMS,
+        cost_estimate=cost(len(far) * rows, count * unit, 0, 2),
+    )(me, *[base] * len(far), sums)
 
 
 def low_rank(extra_ref, start, height, right):
@@ -117,12 +201,10 @@
     out_ref[...] = jnp.sum(total, axis=0, keepdims=True)
 
 
-def sender_squares_kernel(tp, rank, me_ref, *refs):
-    pieces, extras, out_ref = refs[:tp], refs[tp : 2 * tp], refs[-1]
-    start = pl.multiple_of((1 + pl.program_id(0)) * rank, rank)
+def sender_squares_kernel(tp, me_ref, *refs):
+    pieces, rights, left, out_ref = refs[:tp], refs[tp : 2 * tp], refs[-2], refs[-1]
     for d in range(tp):
-        right = extras[d][pl.ds(start, rank), :]
-        total = squares_of(pieces[d], extras[0], right)
+        total = squares_of(pieces[d], left, rights[d][...])
         out_ref[pl.ds(d, 1), :] = jnp.sum(total, axis=0, keepdims=True)
 
 
@@ -136,9 +218,9 @@
         grid_spec=pltpu.PrefetchScalarGridSpec(
             num_scalar_prefetch=1,
             grid=(count,),
-            in_specs=[group_spec(rows, unit, cols // unit, first), chunk_spec(rows, unit, first)]
+            in_specs=[group_spec(rows, unit, cols // unit, first), near_spec(rows, unit, first)]
             + [chunk_spec(rows, unit)] * (tp - 2)
-            + [whole_spec(extra) for extra in extras]
+            + [left_spec(rank, max(rows, BLOCK))] * tp
             + [chunk_spec(rank, unit, first)],
             out_specs=chunk_spec(1, unit),
         ),
@@ -152,18 +234,19 @@
     tp = len(extras)
     groups = base.shape[1] // (tp * unit)
     return pl.pallas_call(
-        functools.partial(sender_squares_kernel, tp, rank),
+        functools.partial(sender_squares_kernel, tp),
         out_shape=jax.ShapeDtypeStruct((tp, count * unit), jnp.float32),
         grid_spec=pltpu.PrefetchScalarGridSpec(
             num_scalar_prefetch=1,
             grid=(count,),
             in_specs=[group_spec(rows, unit, groups, first, d) for d in range(tp)]
-            + [whole_spec(extra) for extra in extras],
+            + [chunk_spec(rank, unit, 1)] * tp
+            + [left_spec(rank, unit)],
             out_specs=chunk_spec(tp, unit),
         ),
         compiler_params=PARAMS,
         cost_estimate=cost(tp * rows, count * unit, rank, 1),
-    )(me, *[base] * tp, *extras)
+    )(me, *[base] * tp, *extras, extras[0])
 
 
 def export_kernel(tp, first, me_ref, *refs):
@@ -210,9 +293,9 @@
         jax.ShapeDtypeStruct((tp * rows // BLOCK, cols // BLOCK), jnp.float32),
     )
     in_specs = (
-        [group_spec(rows, unit, groups, first), chunk_spec(rows, unit, first)]
+        [group_spec(rows, unit, groups, first), near_spec(rows, unit, first)]
         + [chunk_spec(rows, unit)] * (tp - 2)
-        + [whole_spec(extra) for extra in extras]
+        + [left_spec(rank, max(rows, BLOCK))] * tp
         + [chunk_spec(rank, unit, first), chunk_spec(1, unit), group_spec(1, unit, groups, first)]
     )
     args = [base, near, *received, *extras, right, squares, mag]
@@ -245,64 +328,70 @@
     mag = magnitude.reshape(1, -1)
     me = lax.axis_index("tp").astype(jnp.int32).reshape(1)
     early = len(chunks) - LATE
-    late_first = chunks[early][0]
-    late_count = chunks[-1][1] - late_first
+    late = range(chunks[early][0], chunks[-1][1])
     far = range(2, tp)
-
-    late_right = [right[:, u * unit : (u + 1) * unit] for u in range(late_first, late_first + late_count)]
-    own = jnp.concatenate([jnp.pad(left.T, ((0, 0), (0, unit - rows)))] + late_right)
-    me_first = after(me, own)
-    extras = [own, swap(own, 1, tp)]
-    for d in far:
-        extras.append(swap(extras[d - 1], 1, tp) if d % 2 else swap(own, d, tp))
-
     received = {}
 
-    def send(k, me, sums=None):
-        a, b = chunks[k]
-        packed = pack(me, base, tp, far, unit, a, b - a, sums)
-        if k == 1:
-            packed = lax.optimization_barrier((*packed, *received[0]))[: len(far)]
-        received[k] = [swap(piece, d, tp) for d, piece in zip(far, packed)]
-        return packed
-
-    first = send(0, me_first)
-    second = send(1, after(me, *first))
-    near = pack(after(me, *second), base, tp, (1,), unit, 0, cols // unit)[0]
-    near = swap(after(near, extras[-1]), 1, tp)
+    def send(k, pieces):
+        received[k] = [swap(piece, d, tp) for d, piece in zip(far, pieces)]
+
+    *pieces, own = pack_first(me, base, tp, far, left, right, unit, late)
+    send(0, pieces)
+    a, b = chunks[1]
+    pieces = pack(after(me, own), base, tp, far, unit, a, b - a)
+    send(1, pieces)
+    near = lax.all_to_all(
+        pack_near(after(me, *pieces), base, tp), "tp", 0, 0, tiled=True,
+        axis_index_groups=[[i, i + 1] for i in range(0, tp, 2)],
+    )
+
+    even = [own] + [received[0][d - 2][rows:] for d in far[::2]]
+    odd = swap(jnp.concatenate(even), 1, tp)
+    extras = []
+    for i in range(tp // 2):
+        extras += [even[i], odd[i * rank : (i + 1) * rank]]
 
     result = None
-    last = ()
+    token = ()
     totals = {}
-    for k in range(len(chunks)):
-        a, b = chunks[k]
+    waiting = []
+    for k, (a, b) in enumerate(chunks):
         following = k + AHEAD
         if following < len(chunks):
-            token = last if result is None else (*last, result[1])
+            c, d = chunks[following]
             turn = after(me, *received[k], *token)
-            sums = None
             if following == CARRIER:
-                sums = sender_squares(turn, base, extras, rank, unit, late_first, late_count)
-                late = sums[:1] + swap(sums[1:2], 1, tp)
-            send(following, turn, sums)
-        if k < early:
-            local = after(column_squares(me, base, near, received[k], extras, right, unit, a, b - a), *last)
+                sums = sender_squares(turn, base, extras, rank, unit, late[0], len(late))
+                late_sums = sums[:1] + swap(sums[1:2], 1, tp)
+                send(following, pack_carrier(turn, base, tp, far, sums, unit, c, d - c))
+            else:
+                send(following, pack(turn, base, tp, far, unit, c, d - c))
+        waiting.append(k)
+        parts = [i for i in waiting if i < early]
+        if parts:
+            turn = after(me, *token)
+            local = [
+                column_squares(turn, base, near, received[i], extras, right, unit, chunks[i][0], chunks[i][1] - chunks[i][0])
+                for i in parts
+            ]
             if k == CARRIER:
                 for piece in received[k]:
-                    terms = piece[rows : rows + TERMS].astype(jnp.float32)
-                    late = late + jnp.sum(terms, axis=0, keepdims=True)
-                totals[k], late = lax.psum((local, late), "fsdp")
-                for i in range(early, len(chunks)):
-                    start, end = ((u - late_first) * unit for u in chunks[i])
-                    totals[i] = late[:, start:end]
-            else:
-                totals[k] = lax.psum(local, "fsdp")
-            last = (totals[k],)
-        width = unit if k < early else max(unit // 2, BLOCK)
-        parts = unit // width
-        result = export_chunk(
-            me, base, near, received[k], extras, right, totals[k], mag, width, a * parts, (b - a) * parts, result
-        )
+                    terms = after(piece, *token)[rows : rows + TERMS, : late_sums.shape[1]].astype(jnp.float32)
+                    late_sums = late_sums + jnp.sum(terms, axis=0, keepdims=True)
+                local.append(late_sums)
+                parts += range(early, len(chunks))
+            local = jnp.concatenate(local, axis=1)
+            total = lax.psum(local, "fsdp")
+            start = 0
+            for i in parts:
+                end = start + (chunks[i][1] - chunks[i][0]) * unit
+                totals[i] = total[:, start:end]
+                start = end
+        for i in waiting:
+            c, d = chunks[i]
+            result = export_chunk(me, base, near, received[i], extras, right, totals[i], mag, unit, c, d - c, result)
+        waiting = []
+        token = (result[1],)
     return result
 
 

time: 347 us -> 314 us (0.905)
  blocking collectives: 128 us -> 86 us
  waiting for transfers between devices: 84.4 us -> 99.2 us
  Pallas kernels: 106 us -> 99 us
    psum x6 -> x4, blocking collectives: 128 us -> 86 us  [body(): total = lax.psum(local, 'fsdp')]
    all_to_all x0 -> x1, waiting for transfers between devices: none -> 10.4 us  [body(): lax.all_to_all(pack_near(after(me, *pieces), base, tp), 'tp', 0, 0, tiled...]
    all_to_all x0 -> x1, starting transfers between devices: none -> 8.75 us  [body(): lax.all_to_all(pack_near(after(me, *pieces), base, tp), 'tp', 0, 0, tiled...]
    ppermute x21 -> x14, starting transfers between devices: 18.5 us -> 11.9 us  [swap(): return lax.ppermute(array, 'tp', [(i, i ^ d) for i in range(tp)])]
    pallas_call x8 -> x6, Pallas kernels: 45.5 us -> 40.3 us  [export_chunk(): pl.pallas_call(functools.partial(export_kernel, tp, first), out_shape=res...]
    ppermute x21 -> x14, waiting for transfers between devices: 84.4 us -> 88.7 us  [swap(): return lax.ppermute(array, 'tp', [(i, i ^ d) for i in range(tp)])]
    pallas_call x6 -> x4, Pallas kernels: 24.4 us -> 20.7 us  [column_squares(): pl.pallas_call(functools.partial(squares_kernel, tp), out_shape=jax.Shape...]
    pallas_call x10 -> x8, Pallas kernels: 35.8 us -> 38 us  [the longest x4 14.4 us: pack(): pl.pallas_call(functools.partial(copy_kernel, number), out_shape=[jax.Sha...]
  transfers between devices with their start and end apart: 21 -> 15, of which waited for: 7 -> 5; matrix products, arithmetic and copies ran while one was open for 1% -> 2% of each run, Pallas kernels for 29% -> 29%
where the time goes in v4:
time: 314 us; the launch traced here: 313 us
  waiting for transfers between devices  99.2 us (32%)
  Pallas kernels  99 us (32%)
  blocking collectives  86 us (27%)
  starting transfers between devices  20.6 us (7%)
  local copies, waits for them, and re-layouts  3.94 us (1%)
    ppermute x14, waiting for transfers between devices, swap(): return lax.ppermute(array, 'tp', [(i, i ^ d) for i in range(tp)])  88.7 us
    psum x4, blocking collectives, body(): total = lax.psum(local, 'fsdp')  86 us
    pallas_call x6, Pallas kernels, export_chunk(): pl.pallas_call(functools.partial(export_kernel, tp, first), out_shape=res...  40.3 us
    pallas_call x4, Pallas kernels, column_squares(): pl.pallas_call(functools.partial(squares_kernel, tp), out_shape=jax.Shape...  20.7 us
    pallas_call x4, Pallas kernels, pack(): pl.pallas_call(functools.partial(copy_kernel, number), out_shape=[jax.Sha...  14.4 us
    pallas_call x1, Pallas kernels, pack_near(): pl.pallas_call(functools.partial(copy_kernel, 1), out_shape=jax.ShapeDtyp...  12 us
    ppermute x14, starting transfers between devices, swap(): return lax.ppermute(array, 'tp', [(i, i ^ d) for i in range(tp)])  11.9 us
    all_to_all x1, waiting for transfers between devices, body(): lax.all_to_all(pack_near(after(me, *pieces), base, tp), 'tp', 0, 0, tiled...  10.4 us
  transfers between devices with their start and end apart: 15, of which 5 were waited for; matrix products, arithmetic and copies ran while one was open for 2% of the time, Pallas kernels for 29%

profile of v4, /device:TPU:0, one launch (start us, length us, event | category | flops | bytes accessed | tf_op | source)
XLA Modules:
  0.0 312.5 jit_solution(4301947074245818602)
XLA Ops:
  0.6 4.6 %shard_map.59 = (bf16[576,1536]{1,0:T(8,128)(2,1)}, bf16[512,1536]{1,0:T(8,128)(2,1)}, bf16[64,1536]{1,0:T(8,128)(2,1)}) custom-call(s32[1]{0:T(128)} %bitcast.me_ref, bf16[512,26624]{1,0:T(8,128)(2,1)} %refs_0_.35, bf16[512,26624]{1,0:T(8,128)(2,1)} %refs_0_.35, bf16[64,512]{1,0:T(8,128)(2,1)} %bitcast.14, bf16[64,6656]{1,0:T(8,128)(2,1)} %refs_8_.19), custom_call_target="tpu_custom_call" | custom-call | bytes 2097152 | tf_op jit(solution)/shard_map/pallas_call | solution.py:148
  5.2 2.9 collective-permute-start.2
  8.2 4.4 %shard_map.60 = (bf16[512,1536]{1,0:T(8,128)(2,1)}, bf16[512,1536]{1,0:T(8,128)(2,1)}) custom-call(s32[1]{0:T(128)} %bitcast.me_ref, bf16[512,26624]{1,0:T(8,128)(2,1)} %refs_0_.35, bf16[512,26624]{1,0:T(8,128)(2,1)} %refs_0_.35), custom_call_target="tpu_custom_call" | custom-call | bytes 2097152 | tf_op jit(solution)/shard_map/pallas_call | solution.py:106
  14.4 33.5 %collective-permute-done.2.refs_2_ = bf16[576,1536]{1,0:T(8,128)(2,1)S(1)} collective-permute-done((bf16[576,1536]{1,0:T(8,128)(2,1)}, bf16[576,1536]{1,0:T(8,128)(2,1)S(1)}, u32[]{:S(2)}, u32[]{:S(2)}) %collective-permute-start.2) | collective-permute-done | bytes 1769504 | tf_op jit(solution)/shard_map/ppermute | solution.py:35
  48.7 32.5 %collective-permute-done.3.refs_3_ = bf16[512,1536]{1,0:T(8,128)(2,1)S(1)} collective-permute-done((bf16[512,1536]{1,0:T(8,128)(2,1)}, bf16[512,1536]{1,0:T(8,128)(2,1)S(1)}, u32[]{:S(2)}, u32[]{:S(2)}) %collective-permute-start.3) | collective-permute-done | bytes 1572896 | tf_op jit(solution)/shard_map/ppermute | solution.py:35
  81.2 4.9 %shard_map.66 = (bf16[512,1536]{1,0:T(8,128)(2,1)}, bf16[512,1536]{1,0:T(8,128)(2,1)}) custom-call(s32[1]{0:T(128)} %bitcast.me_ref, bf16[512,26624]{1,0:T(8,128)(2,1)} %refs_0_.35, bf16[512,26624]{1,0:T(8,128)(2,1)} %refs_0_.35), custom_call_target="tpu_custom_call" | custom-call | bytes 2097152 | tf_op jit(solution)/shard_map/pallas_call | solution.py:106
  86.3 1.8 collective-permute-start.8
  88.1 12.0 %shard_map.61 = bf16[1024,6656]{1,0:T(8,128)(2,1)} custom-call(s32[1]{0:T(128)} %bitcast.me_ref, bf16[512,26624]{1,0:T(8,128)(2,1)} %refs_0_.35), custom_call_target="tpu_custom_call" | custom-call | bytes 4543829 | tf_op jit(solution)/shard_map/pallas_call | solution.py:125
  100.1 8.8 %all-to-all-start = ((bf16[2,512,6656]{2,1,0:T(8,128)(2,1)}), bf16[2,512,6656]{2,1,0:T(8,128)(2,1)}, u32[]{:S(2)}, u32[]{:S(2)}) async-start(bf16[2,512,6656]{2,1,0:T(8,128)(2,1)} %bitcast.7), calls=%async_computation | async-start | bytes 27262976 | tf_op jit(solution)/shard_map/all_to_all | solution.py:343
  109.6 10.4 %all-to-all-done = bf16[2,512,6656]{2,1,0:T(8,128)(2,1)} async-done(((bf16[2,512,6656]{2,1,0:T(8,128)(2,1)}), bf16[2,512,6656]{2,1,0:T(8,128)(2,1)}, u32[]{:S(2)}, u32[]{:S(2)}) %all-to-all-start) | async-done | bytes 13631520 | tf_op jit(solution)/shard_map/all_to_all | solution.py:343
  120.1 5.5 %shard_map.62 = f32[1,1536]{1,0:T(1,128)} custom-call(s32[1]{0:T(128)} %bitcast.me_ref, bf16[512,26624]{1,0:T(8,128)(2,1)} %refs_0_.35, bf16[1024,6656]{1,0:T(8,128)(2,1)} %bitcast.3.refs_1_, bf16[576,1536]{1,0:T(8,128)(2,1)} %copy-done.2, bf16[512,1536]{1,0:T(8,128)(2,1)} %copy-done.3, bf16[64,1536]{1,0:T(8,128)(2,1)} %get-tuple-element.36.refs_4_.refs_8_, ...), custom_call_target="tpu_custom_call" | custom-call | flops 134217728 | bytes 2097152 | tf_op jit(solution)/shard_map/pallas_call | solution.py:215
  125.6 22.8 %psum.28.refs_9_ = f32[1,1536]{1,0:T(1,128)} all-reduce(f32[1,1536]{1,0:T(1,128)} %shard_map.62), channel_id=1, replica_groups=mesh['fsdp'=8,'tp'=4] {'fsdp'}, use_global_device_ids=true, to_apply=%region_0.0 | all-reduce | flops 1536 | bytes 12288 | tf_op jit(solution)/shard_map/psum | solution.py:384
  148.4 8.4 %shard_map.63 = (bf16[2048,6656]{1,0:T(8,128)(2,1)}, f32[16,52]{1,0:T(8,128)}) custom-call(s32[1]{0:T(128)} %bitcast.me_ref, bf16[512,26624]{1,0:T(8,128)(2,1)} %refs_0_.35, bf16[1024,6656]{1,0:T(8,128)(2,1)} %bitcast.3.refs_1_, bf16[576,1536]{1,0:T(8,128)(2,1)} %copy-done.2, bf16[512,1536]{1,0:T(8,128)(2,1)} %copy-done.3, ...), custom_call_target="tpu_custom_call" | custom-call | flops 134217728 | bytes 4194304 | tf_op jit(solution)/shard_map/pallas_call | solution.py:307
  156.9 4.2 %shard_map.64.refs_2_ = f32[4,1024]{1,0:T(4,128)} custom-call(s32[1]{0:T(128)} %bitcast.me_ref, bf16[512,26624]{1,0:T(8,128)(2,1)} %refs_0_.35, bf16[512,26624]{1,0:T(8,128)(2,1)} %refs_0_.35, bf16[512,26624]{1,0:T(8,128)(2,1)} %refs_0_.35, bf16[512,26624]{1,0:T(8,128)(2,1)} %refs_0_.35, bf16[64,1536]{1,0:T(8,128)(2,1)} %get-tuple-element.36.refs_4_.refs_8_, ...), custom_call_target="tpu_custom_call" | custom-call | flops 89478488 | bytes 1398101 | tf_op jit(solution)/shard_map/pallas_call | solution.py:236
  161.1 2.8 shard_map.65
  165.3 5.6 %shard_map.67 = f32[1,1536]{1,0:T(1,128)} custom-call(s32[1]{0:T(128)} %bitcast.me_ref, bf16[512,26624]{1,0:T(8,128)(2,1)} %refs_0_.35, bf16[1024,6656]{1,0:T(8,128)(2,1)} %bitcast.3.refs_1_, bf16[512,1536]{1,0:T(8,128)(2,1)} %collective-permute-done.refs_2_, bf16[512,1536]{1,0:T(8,128)(2,1)} %collective-permute-done.1.refs_3_, ...), custom_call_target="tpu_custom_call" | custom-call | flops 134217728 | bytes 2097152 | tf_op jit(solution)/shard_map/pallas_call | solution.py:215
  170.9 18.1 %psum.29.refs_9_ = f32[1,1536]{1,0:T(1,128)} all-reduce(f32[1,1536]{1,0:T(1,128)} %shard_map.67), channel_id=1, replica_groups=mesh['fsdp'=8,'tp'=4] {'fsdp'}, use_global_device_ids=true, to_apply=%region_1.0 | all-reduce | flops 1536 | bytes 12288 | tf_op jit(solution)/shard_map/psum | solution.py:384
  189.0 8.4 %shard_map.68 = (bf16[2048,6656]{1,0:T(8,128)(2,1)}, f32[16,52]{1,0:T(8,128)}) custom-call(s32[1]{0:T(128)} %bitcast.me_ref, bf16[512,26624]{1,0:T(8,128)(2,1)} %refs_0_.35, bf16[1024,6656]{1,0:T(8,128)(2,1)} %bitcast.3.refs_1_, bf16[512,1536]{1,0:T(8,128)(2,1)} %collective-permute-done.refs_2_, ...), custom_call_target="tpu_custom_call", output_to_operand_aliasing={{0}: (12, {})} | custom-call | flops 134217728 | bytes 4194304 | tf_op jit(solution)/shard_map/pallas_call | solution.py:307
  197.5 18.6 %collective-permute-done.8.refs_3_ = bf16[512,1536]{1,0:T(8,128)(2,1)S(1)} collective-permute-done((bf16[512,1536]{1,0:T(8,128)(2,1)}, bf16[512,1536]{1,0:T(8,128)(2,1)S(1)}, u32[]{:S(2)}, u32[]{:S(2)}) %collective-permute-start.8) | collective-permute-done | bytes 1572896 | tf_op jit(solution)/shard_map/ppermute | solution.py:35
  216.0 2.8 shard_map.73
  218.9 1.8 collective-permute-start.13
  220.7 5.5 %shard_map.69 = f32[1,1536]{1,0:T(1,128)} custom-call(s32[1]{0:T(128)} %bitcast.me_ref, bf16[512,26624]{1,0:T(8,128)(2,1)} %refs_0_.35, bf16[1024,6656]{1,0:T(8,128)(2,1)} %bitcast.3.refs_1_, bf16[512,1536]{1,0:T(8,128)(2,1)} %copy-done.4, bf16[512,1536]{1,0:T(8,128)(2,1)} %copy-done.5, bf16[64,1536]{1,0:T(8,128)(2,1)} %get-tuple-element.36.refs_4_.refs_8_, ...), custom_call_target="tpu_custom_call" | custom-call | flops 134217728 | bytes 2097152 | tf_op jit(solution)/shard_map/pallas_call | solution.py:215
  226.3 22.8 %psum.30.refs_9_ = f32[1,1536]{1,0:T(1,128)} all-reduce(f32[1,1536]{1,0:T(1,128)} %shard_map.69), channel_id=1, replica_groups=mesh['fsdp'=8,'tp'=4] {'fsdp'}, use_global_device_ids=true, to_apply=%region_2.0 | all-reduce | flops 1536 | bytes 12288 | tf_op jit(solution)/shard_map/psum | solution.py:384
  249.1 8.4 %shard_map.70 = (bf16[2048,6656]{1,0:T(8,128)(2,1)}, f32[16,52]{1,0:T(8,128)}) custom-call(s32[1]{0:T(128)} %bitcast.me_ref, bf16[512,26624]{1,0:T(8,128)(2,1)} %refs_0_.35, bf16[1024,6656]{1,0:T(8,128)(2,1)} %bitcast.3.refs_1_, bf16[512,1536]{1,0:T(8,128)(2,1)} %copy-done.4, bf16[512,1536]{1,0:T(8,128)(2,1)} %copy-done.5, ...), custom_call_target="tpu_custom_call", output_to_operand_aliasing={{0}: (12, {})} | custom-call | flops 134217728 | bytes 4194304 | tf_op jit(solution)/shard_map/pallas_call | solution.py:307
  258.3 4.1 %collective-permute-done.6.refs_3_ = bf16[528,1024]{1,0:T(8,128)(2,1)} collective-permute-done((bf16[528,1024]{1,0:T(8,128)(2,1)}, bf16[528,1024]{1,0:T(8,128)(2,1)}, u32[]{:S(2)}, u32[]{:S(2)}) %collective-permute-start.6) | collective-permute-done | bytes 1081376 | tf_op jit(solution)/shard_map/ppermute | solution.py:35
  263.1 2.2 shard_map.71
  265.6 1.8 collective-permute-start.10
  267.3 4.1 %shard_map.72 = f32[1,1024]{1,0:T(1,128)} custom-call(s32[1]{0:T(128)} %bitcast.me_ref, bf16[512,26624]{1,0:T(8,128)(2,1)} %refs_0_.35, bf16[1024,6656]{1,0:T(8,128)(2,1)} %bitcast.3.refs_1_, bf16[528,1024]{1,0:T(8,128)(2,1)} %collective-permute-done.5.refs_2_, bf16[528,1024]{1,0:T(8,128)(2,1)} %collective-permute-done.6.refs_3_, ...), custom_call_target="tpu_custom_call" | custom-call | flops 89478488 | bytes 1398101 | tf_op jit(solution)/shard_map/pallas_call | solution.py:215
  272.1 22.3 %psum.31 = f32[1,2048]{1,0:T(1,128)S(1)} all-reduce(f32[1,2048]{1,0:T(1,128)S(1)} %pad_maximum_fusion.1), channel_id=1, replica_groups=mesh['fsdp'=8,'tp'=4] {'fsdp'}, use_global_device_ids=true, to_apply=%region_5.0 | all-reduce | flops 2048 | bytes 16384 | tf_op jit(solution)/shard_map/psum | solution.py:384
  295.0 6.2 %shard_map.74 = (bf16[2048,6656]{1,0:T(8,128)(2,1)}, f32[16,52]{1,0:T(8,128)}) custom-call(s32[1]{0:T(128)} %bitcast.me_ref, bf16[512,26624]{1,0:T(8,128)(2,1)} %refs_0_.35, bf16[1024,6656]{1,0:T(8,128)(2,1)} %bitcast.3.refs_1_, bf16[528,1024]{1,0:T(8,128)(2,1)} %collective-permute-done.5.refs_2_, ...), custom_call_target="tpu_custom_call", output_to_operand_aliasing={{0}: (12, {})} | custom-call | flops 89478488 | bytes 2796202 | tf_op jit(solution)/shard_map/pallas_call | solution.py:307
  302.8 4.4 %shard_map.75 = (bf16[2048,6656]{1,0:T(8,128)(2,1)}, f32[16,52]{1,0:T(8,128)}) custom-call(s32[1]{0:T(128)} %bitcast.me_ref, bf16[512,26624]{1,0:T(8,128)(2,1)} %refs_0_.35, bf16[1024,6656]{1,0:T(8,128)(2,1)} %bitcast.3.refs_1_, bf16[512,512]{1,0:T(8,128)(2,1)} %copy-done.6, bf16[512,512]{1,0:T(8,128)(2,1)} %copy-done.7, ...), custom_call_target="tpu_custom_call", output_to_operand_aliasing={{0}: (12, {})} | custom-call | flops 44739240 | bytes 1398101 | tf_op jit(solution)/shard_map/pallas_call | solution.py:307
  308.2 4.3 %shard_map.76 = (bf16[2048,6656]{1,0:T(8,128)(2,1)}, f32[16,52]{1,0:T(8,128)}) custom-call(s32[1]{0:T(128)} %bitcast.me_ref, bf16[512,26624]{1,0:T(8,128)(2,1)} %refs_0_.35, bf16[1024,6656]{1,0:T(8,128)(2,1)} %bitcast.3.refs_1_, bf16[512,512]{1,0:T(8,128)(2,1)} %copy-done.8, bf16[512,512]{1,0:T(8,128)(2,1)} %copy-done.9, ...), custom_call_target="tpu_custom_call", output_to_operand_aliasing={{0}: (12, {})} | custom-call | flops 44739240 | bytes 1398101 | tf_op jit(solution)/shard_map/pallas_call | solution.py:307
  (52 shorter events, 10.5 us)
Async XLA Ops:
  5.2 42.6 %collective-permute-start.2 = (bf16[576,1536]{1,0:T(8,128)(2,1)}, bf16[576,1536]{1,0:T(8,128)(2,1)S(1)}, u32[]{:S(2)}, u32[]{:S(2)}) collective-permute-start(bf16[576,1536]{1,0:T(8,128)(2,1)} %get-tuple-element.41), channel_id=1, source_target_pairs={{0,2},{1,3},{2,0},{3,1},{4,6},{5,7},{6,4},{7,5},{8,10},{9,11},{10,... | collective-permute-start | bytes 5308424 | tf_op jit(solution)/shard_map/ppermute | solution.py:35
  8.2 73.0 %collective-permute-start.3 = (bf16[512,1536]{1,0:T(8,128)(2,1)}, bf16[512,1536]{1,0:T(8,128)(2,1)S(1)}, u32[]{:S(2)}, u32[]{:S(2)}) collective-permute-start(bf16[512,1536]{1,0:T(8,128)(2,1)} %get-tuple-element.42), channel_id=1, source_target_pairs={{0,3},{1,2},{2,1},{3,0},{4,7},{5,6},{6,5},{7,4},{8,11},{9,10},{10,... | collective-permute-start | bytes 4718600 | tf_op jit(solution)/shard_map/ppermute | solution.py:35
  8.2 39.7 %copy-start = (bf16[64,1536]{1,0:T(8,128)(2,1)S(1)}, bf16[64,1536]{1,0:T(8,128)(2,1)}, u32[]{:S(2)}) copy-start(bf16[64,1536]{1,0:T(8,128)(2,1)} %get-tuple-element.36.refs_4_.refs_8_) | copy-start | bytes 589828
  12.6 144.3 %collective-permute-start = (bf16[512,1536]{1,0:T(8,128)(2,1)}, bf16[512,1536]{1,0:T(8,128)(2,1)}, u32[]{:S(2)}, u32[]{:S(2)}) collective-permute-start(bf16[512,1536]{1,0:T(8,128)(2,1)} %get-tuple-element.38), channel_id=1, source_target_pairs={{0,2},{1,3},{2,0},{3,1},{4,6},{5,7},{6,4},{7,5},{8,10},{9,11},{10,... | collective-permute-start | bytes 4718600 | tf_op jit(solution)/shard_map/ppermute | solution.py:35
  13.8 143.1 %collective-permute-start.1 = (bf16[512,1536]{1,0:T(8,128)(2,1)}, bf16[512,1536]{1,0:T(8,128)(2,1)}, u32[]{:S(2)}, u32[]{:S(2)}) collective-permute-start(bf16[512,1536]{1,0:T(8,128)(2,1)} %get-tuple-element.39), channel_id=1, source_target_pairs={{0,3},{1,2},{2,1},{3,0},{4,7},{5,6},{6,5},{7,4},{8,11},{9,10},{10,... | collective-permute-start | bytes 4718600 | tf_op jit(solution)/shard_map/ppermute | solution.py:35
  47.8 38.3 %copy-start.2 = (bf16[576,1536]{1,0:T(8,128)(2,1)}, bf16[576,1536]{1,0:T(8,128)(2,1)S(1)}, u32[]{:S(2)}) copy-start(bf16[576,1536]{1,0:T(8,128)(2,1)S(1)} %collective-permute-done.2.refs_2_) | copy-start | bytes 5308420
  47.9 38.3 %copy-start.1 = (bf16[64,1536]{1,0:T(8,128)(2,1)}, bf16[64,1536]{1,0:T(8,128)(2,1)S(1)}, u32[]{:S(2)}) copy-start(bf16[64,1536]{1,0:T(8,128)(2,1)S(1)} %slice.40.refs_6_) | copy-start | bytes 589828
  48.7 60.2 %collective-permute-start.4 = (bf16[128,1536]{1,0:T(8,128)(2,1)}, bf16[128,1536]{1,0:T(8,128)(2,1)S(1)}, u32[]{:S(2)}, u32[]{:S(2)}) collective-permute-start(bf16[128,1536]{1,0:T(8,128)(2,1)} %pad_maximum_fusion), channel_id=1, source_target_pairs={{0,1},{1,0},{2,3},{3,2},{4,5},{5,4},{6,7},{7,6},{8,9},{9,8},{10,11... | collective-permute-start | bytes 1179656 | tf_op jit(solution)/shard_map/ppermute | solution.py:35
  81.2 4.9 %copy-start.3 = (bf16[512,1536]{1,0:T(8,128)(2,1)}, bf16[512,1536]{1,0:T(8,128)(2,1)S(1)}, u32[]{:S(2)}) copy-start(bf16[512,1536]{1,0:T(8,128)(2,1)S(1)} %collective-permute-done.3.refs_3_) | copy-start | bytes 4718596
  86.2 111.3 %collective-permute-start.7 = (bf16[512,1536]{1,0:T(8,128)(2,1)}, bf16[512,1536]{1,0:T(8,128)(2,1)S(1)}, u32[]{:S(2)}, u32[]{:S(2)}) collective-permute-start(bf16[512,1536]{1,0:T(8,128)(2,1)} %get-tuple-element.48), channel_id=1, source_target_pairs={{0,2},{1,3},{2,0},{3,1},{4,6},{5,7},{6,4},{7,5},{8,10},{9,11},{10,... | collective-permute-start | bytes 4718600 | tf_op jit(solution)/shard_map/ppermute | solution.py:35
  86.3 129.7 %collective-permute-start.8 = (bf16[512,1536]{1,0:T(8,128)(2,1)}, bf16[512,1536]{1,0:T(8,128)(2,1)S(1)}, u32[]{:S(2)}, u32[]{:S(2)}) collective-permute-start(bf16[512,1536]{1,0:T(8,128)(2,1)} %get-tuple-element.49), channel_id=1, source_target_pairs={{0,3},{1,2},{2,1},{3,0},{4,7},{5,6},{6,5},{7,4},{8,11},{9,10},{10,... | collective-permute-start | bytes 4718600 | tf_op jit(solution)/shard_map/ppermute | solution.py:35
  100.1 20.0 %all-to-all-start = ((bf16[2,512,6656]{2,1,0:T(8,128)(2,1)}), bf16[2,512,6656]{2,1,0:T(8,128)(2,1)}, u32[]{:S(2)}, u32[]{:S(2)}) async-start(bf16[2,512,6656]{2,1,0:T(8,128)(2,1)} %bitcast.7), calls=%async_computation | async-start | bytes 27262976 | tf_op jit(solution)/shard_map/all_to_all | solution.py:343
  161.1 4.2 %copy-start.10 = (f32[4,1024]{1,0:T(4,128)S(1)}, f32[4,1024]{1,0:T(4,128)}, u32[]{:S(2)}) copy-start(f32[4,1024]{1,0:T(4,128)} %shard_map.64.refs_2_) | copy-start | bytes 49156
  163.9 93.6 %collective-permute-start.5 = (bf16[528,1024]{1,0:T(8,128)(2,1)}, bf16[528,1024]{1,0:T(8,128)(2,1)}, u32[]{:S(2)}, u32[]{:S(2)}) collective-permute-start(bf16[528,1024]{1,0:T(8,128)(2,1)} %get-tuple-element.45), channel_id=1, source_target_pairs={{0,2},{1,3},{2,0},{3,1},{4,6},{5,7},{6,4},{7,5},{8,10},{9,11},{10,... | collective-permute-start | bytes 3244040 | tf_op jit(solution)/shard_map/ppermute | solution.py:35
  165.3 97.1 %collective-permute-start.6 = (bf16[528,1024]{1,0:T(8,128)(2,1)}, bf16[528,1024]{1,0:T(8,128)(2,1)}, u32[]{:S(2)}, u32[]{:S(2)}) collective-permute-start(bf16[528,1024]{1,0:T(8,128)(2,1)} %get-tuple-element.46), channel_id=1, source_target_pairs={{0,3},{1,2},{2,1},{3,0},{4,7},{5,6},{6,5},{7,4},{8,11},{9,10},{10,... | collective-permute-start | bytes 3244040 | tf_op jit(solution)/shard_map/ppermute | solution.py:35
  197.4 69.9 %collective-permute-start.11 = (f32[1,1024]{1,0:T(1,128)S(1)}, f32[1,1024]{1,0:T(1,128)S(1)}, u32[]{:S(2)}, u32[]{:S(2)}) collective-permute-start(f32[1,1024]{1,0:T(1,128)S(1)} %slice.44), channel_id=1, source_target_pairs={{0,1},{1,0},{2,3},{3,2},{4,5},{5,4},{6,7},{7,6},{8,9},{9,8},{10,11... | collective-permute-start | bytes 12296 | tf_op jit(solution)/shard_map/ppermute | solution.py:35
  197.4 21.4 %copy-start.4 = (bf16[512,1536]{1,0:T(8,128)(2,1)}, bf16[512,1536]{1,0:T(8,128)(2,1)S(1)}, u32[]{:S(2)}) copy-start(bf16[512,1536]{1,0:T(8,128)(2,1)S(1)} %collective-permute-done.7.refs_2_) | copy-start | bytes 4718596
  216.0 2.8 copy-start.5
  218.9 83.0 %collective-permute-start.12 = (bf16[512,512]{1,0:T(8,128)(2,1)}, bf16[512,512]{1,0:T(8,128)(2,1)S(1)}, u32[]{:S(2)}, u32[]{:S(2)}) collective-permute-start(bf16[512,512]{1,0:T(8,128)(2,1)} %get-tuple-element.63), channel_id=1, source_target_pairs={{0,2},{1,3},{2,0},{3,1},{4,6},{5,7},{6,4},{7,5},{8,10},{9,11},{10,... | collective-permute-start | bytes 1572872 | tf_op jit(solution)/shard_map/ppermute | solution.py:35
  218.9 82.9 %collective-permute-start.13 = (bf16[512,512]{1,0:T(8,128)(2,1)}, bf16[512,512]{1,0:T(8,128)(2,1)S(1)}, u32[]{:S(2)}, u32[]{:S(2)}) collective-permute-start(bf16[512,512]{1,0:T(8,128)(2,1)} %get-tuple-element.64), channel_id=1, source_target_pairs={{0,3},{1,2},{2,1},{3,0},{4,7},{5,6},{6,5},{7,4},{8,11},{9,10},{10,... | collective-permute-start | bytes 1572872 | tf_op jit(solution)/shard_map/ppermute | solution.py:35
  265.4 41.8 %collective-permute-start.9 = (bf16[512,512]{1,0:T(8,128)(2,1)}, bf16[512,512]{1,0:T(8,128)(2,1)S(1)}, u32[]{:S(2)}, u32[]{:S(2)}) collective-permute-start(bf16[512,512]{1,0:T(8,128)(2,1)} %get-tuple-element.57), channel_id=1, source_target_pairs={{0,2},{1,3},{2,0},{3,1},{4,6},{5,7},{6,4},{7,5},{8,10},{9,11},{10,... | collective-permute-start | bytes 1572872 | tf_op jit(solution)/shard_map/ppermute | solution.py:35
  265.6 41.7 %collective-permute-start.10 = (bf16[512,512]{1,0:T(8,128)(2,1)}, bf16[512,512]{1,0:T(8,128)(2,1)S(1)}, u32[]{:S(2)}, u32[]{:S(2)}) collective-permute-start(bf16[512,512]{1,0:T(8,128)(2,1)} %get-tuple-element.58), channel_id=1, source_target_pairs={{0,3},{1,2},{2,1},{3,0},{4,7},{5,6},{6,5},{7,4},{8,11},{9,10},{10,... | collective-permute-start | bytes 1572872 | tf_op jit(solution)/shard_map/ppermute | solution.py:35
  301.8 0.8 copy-start.6
  301.9 1.0 copy-start.7
  307.2 0.8 copy-start.8
  307.2 1.0 copy-start.9
